TPU v7x, 32 devices: a whole 2x2x4 slice. The times are simulated.
32 devices in a mesh: out: 8 (over y, x, core), in: 4 (over z).
Axes of the slice: x: 2, y: 2, z: 4, core: 2. Of those that a mesh axis runs over, the one named last changes fastest.
Arguments:
- activations: bfloat16 [512, 8192], P('in', 'out'), may hold values from -6 to 6
- out_grad: bfloat16 [512, 28672], P('out', 'in'), may hold values from -6 to 6
- basis_out: bfloat16 [28672, 28672], P('in', 'out'), may hold values from -0.03125 to 0.03125
- basis_in: bfloat16 [8192, 8192], P('out', 'in'), may hold values from -0.0625 to 0.0625
- eigenvalues: bfloat16 [28672, 8192], P('out', 'in'), may hold values from 0.5 to 8
- query_out: bfloat16 [256, 28672], P(None, 'in'), may hold values from -0.0078125 to 0.0078125
- query_in: bfloat16 [256, 8192], P(None, 'out'), may hold values from -0.015625 to 0.015625
- query_domain: int32 [32], replicated, may hold values from 0 to 7
- seq_weight: int32 [4, 8], replicated, may hold values from 1 to 16
Outputs:
- mixed: bfloat16 [28672, 8192], P('out', 'in')
- influence: float32 [4, 32], replicated
All inputs are finite; a program needn't handle non-finite values.
Results may differ from a plain program's by a relative error of at most 0.0065.
Values may be sent and summed in bfloat16 or wider, within the bound.
No kernel may reach another device: no remote copies, remote signals or barrier semaphores. Data moves between devices by JAX's collectives and lax.ppermute only.
A program may use at most 256 MiB of HBM per device.

v0:
```python
import math

import jax
import jax.numpy as jnp
from jax import lax
from jax.sharding import PartitionSpec as P

SEQS = 4
LEN = 128
QUERIES = 32
RANK = 8
DOMAINS = 8


def on_device(
    activations,
    out_grad,
    basis_out,
    basis_in,
    eigenvalues,
    query_out,
    query_in,
    query_domain,
    seq_weight,
):
    tokens = SEQS * LEN
    grad_rows = lax.all_gather(out_grad, "out", axis=0, tiled=True)
    act_rows = lax.all_gather(activations, "in", axis=0, tiled=True)
    grad_stack = jnp.concatenate([grad_rows, query_out], axis=0)
    act_stack = jnp.concatenate([act_rows, query_in], axis=0)
    picked_rows = grad_stack
    grad_part = lax.psum_scatter(
        jnp.dot(picked_rows, basis_out, preferred_element_type=jnp.float32),
        "in",
        scatter_dimension=0,
        tiled=True,
    )
    grad_rotated = lax.all_gather(grad_part.astype(jnp.bfloat16), "in", axis=0, tiled=True)
    picked_rows = act_stack
    act_part = lax.psum_scatter(
        jnp.dot(picked_rows, basis_in, preferred_element_type=jnp.float32),
        "out",
        scatter_dimension=0,
        tiled=True,
    )
    act_rotated = lax.all_gather(act_part.astype(jnp.bfloat16), "out", axis=0, tiled=True)
    rot_grad = grad_rotated[:tokens]
    rot_qout = grad_rotated[tokens:]
    rot_act = act_rotated[:tokens]
    rot_qin = act_rotated[tokens:]
    eigen_local = eigenvalues.astype(jnp.float32)
    qout_float = rot_qout.astype(jnp.float32)
    accumulated = jnp.zeros(eigen_local.shape, jnp.float32)
    partials = []
    for sequence in range(SEQS):
        lower = sequence * LEN
        grad_block = rot_grad[lower : lower + LEN]
        act_block = rot_act[lower : lower + LEN]
        rotated = lax.dot_general(
            grad_block, act_block, (((0,), (0,)), ((), ())), preferred_element_type=jnp.float32
        )
        precond = rotated / eigen_local
        accumulated = accumulated + precond
        projected = lax.dot_general(
            rot_qin,
            precond.astype(jnp.bfloat16),
            (((1,), (1,)), ((), ())),
            preferred_element_type=jnp.float32,
        )
        per_factor = jnp.sum(projected * qout_float, axis=1)
        partials.append(jnp.sum(per_factor.reshape(QUERIES, RANK), axis=1))
    local_scores = jnp.stack(partials)
    score = lax.psum(local_scores, ("out", "in"))
    mixed = (accumulated * (1.0 / math.sqrt(SEQS * LEN))).astype(jnp.bfloat16)
    weights = seq_weight.astype(jnp.float32)
    onehot = (query_domain[:, None] == jnp.arange(DOMAINS, dtype=jnp.int32)[None, :]).astype(
        jnp.float32
    )
    picked = jnp.sum(weights[:, None, :] * onehot[None, :, :], axis=2)
    mean_weight = jnp.sum(weights, axis=1, keepdims=True) / DOMAINS
    influence = score * picked / mean_weight
    return (mixed, influence)


def solution(mesh):
    return jax.shard_map(
        on_device,
        mesh=mesh,
        in_specs=(
            P("in", "out"),
            P("out", "in"),
            P("in", "out"),
            P("out", "in"),
            P("out", "in"),
            P(None, "in"),
            P(None, "out"),
            P(),
            P(),
        ),
        out_specs=(P("out", "in"), P()),
        check_vma=False,
    )
```

profile of v0, /device:TPU:0, one launch (start us, length us, event | category | flops | bytes accessed | tf_op | source)
XLA Modules:
  0.0 674.2 jit_solution(8563261908907233936)
XLA Ops:
  7.2 0.7 all-gather.9.cloned.1.call-update
  7.9 0.7 all-gather.5.cloned.1.call-update
  8.7 31.5 %all-gather.9.cloned.1.call-done = bf16[512,1024]{1,0:T(8,128)(2,1)} async-done(((bf16[128,1024]{1,0:T(8,128)(2,1)}), bf16[512,1024]{1,0:T(8,128)(2,1)}) %all-gather.9.cloned.1.call-update) | async-done | bytes 1048592 | tf_op jit(solution)/shard_map/all_gather | solution.py:28
  40.2 8.8 %fusion.20 = f32[768,2048]{1,0:T(8,128)} fusion(bf16[1024,2048]{1,0:T(8,128)(2,1)} %param.12, bf16[256,1024]{1,0:T(8,128)(2,1)} %param.15, bf16[512,1024]{1,0:T(8,128)(2,1)} %all-gather.9.cloned.1.call-done), kind=kOutput, calls=%fused_computation.21 | convolution fusion | flops 3224371200 | bytes 12058624 | tf_op jit(solution)/shard_map/dot_general | solution.py:41
  49.1 42.5 %all-gather.5.cloned.1.call-done = bf16[512,7168]{1,0:T(8,128)(2,1)} async-done(((bf16[64,7168]{1,0:T(8,128)(2,1)}), bf16[512,7168]{1,0:T(8,128)(2,1)}) %all-gather.5.cloned.1.call-update) | async-done | bytes 7340048 | tf_op jit(solution)/shard_map/all_gather | solution.py:27
  91.6 48.3 %fusion.8 = f32[768,3584]{1,0:T(8,128)} fusion(bf16[7168,3584]{1,0:T(8,128)(2,1)} %param.11, bf16[256,7168]{1,0:T(8,128)(2,1)} %param.14, bf16[512,7168]{1,0:T(8,128)(2,1)} %all-gather.5.cloned.1.call-done), kind=kOutput, calls=%fused_computation.13 | convolution fusion | flops 39482032128 | bytes 73400320 | tf_op jit(solution)/shard_map/dot_general | solution.py:33
  140.0 16.8 %reduce-scatter.5.cloned.1.call-done = f32[96,2048]{1,0:T(8,128)} async-done(((f32[768,2048]{1,0:T(8,128)}), f32[96,2048]{1,0:T(8,128)}) %reduce-scatter.5.cloned.1.call-update) | async-done | bytes 786448 | tf_op jit(solution)/shard_map/reduce_scatter | solution.py:40
  156.8 1.9 convert_element_type.38
  159.0 187.2 %reduce-scatter.3.cloned.1.call-done = f32[192,3584]{1,0:T(8,128)} async-done(((f32[768,3584]{1,0:T(8,128)}), f32[192,3584]{1,0:T(8,128)}) %reduce-scatter.3.cloned.1.call-update) | async-done | bytes 2752528 | tf_op jit(solution)/shard_map/reduce_scatter | solution.py:32
  346.2 3.0 convert_element_type.37
  349.3 0.7 multiply_reduce_fusion
  350.0 0.6 broadcast_multiply_fusion
  350.6 30.9 %all-gather.11.cloned.1.call-done = bf16[768,2048]{1,0:T(8,128)(2,1)} async-done(((bf16[96,2048]{1,0:T(8,128)(2,1)}), bf16[768,2048]{1,0:T(8,128)(2,1)}) %all-gather.11.cloned.1.call-update) | async-done | bytes 3145744 | tf_op jit(solution)/shard_map/all_gather | solution.py:46
  381.5 104.5 %all-gather.7.cloned.1.call-done = bf16[768,3584]{1,0:T(8,128)(2,1)} async-done(((bf16[192,3584]{1,0:T(8,128)(2,1)}), bf16[768,3584]{1,0:T(8,128)(2,1)}) %all-gather.7.cloned.1.call-update) | async-done | bytes 5505040 | tf_op jit(solution)/shard_map/all_gather | solution.py:38
  486.0 15.6 %convert_divide_fusion.1 = f32[3584,2048]{1,0:T(8,128)} fusion(bf16[3584,2048]{1,0:T(8,128)(2,1)} %param.13, bf16[768,3584]{1,0:T(8,128)(2,1)} %all-gather.7.cloned.1.call-done, bf16[768,2048]{1,0:T(8,128)(2,1)} %all-gather.11.cloned.1.call-done), kind=kOutput, calls=%fused_computation.1 | convolution fusion | flops 1893728256 | bytes 45481984 | tf_op jit(solution)/shard_map/dot_general | solution.py:59
  501.6 14.8 %convert_divide_fusion.3 = f32[3584,2048]{1,0:T(8,128)} fusion(bf16[3584,2048]{1,0:T(8,128)(2,1)} %param.13, bf16[768,3584]{1,0:T(8,128)(2,1)S(1)} %copy-done.1, bf16[768,2048]{1,0:T(8,128)(2,1)S(1)} %copy-done), kind=kOutput, calls=%fused_computation.3 | convolution fusion | flops 1893728256 | bytes 45481984 | tf_op jit(solution)/shard_map/dot_general | solution.py:59
  516.4 14.7 %convert_divide_fusion.2 = f32[3584,2048]{1,0:T(8,128)} fusion(bf16[3584,2048]{1,0:T(8,128)(2,1)} %param.13, bf16[768,3584]{1,0:T(8,128)(2,1)S(1)} %copy-done.1, bf16[768,2048]{1,0:T(8,128)(2,1)S(1)} %copy-done), kind=kOutput, calls=%fused_computation.2 | convolution fusion | flops 1893728256 | bytes 45481984 | tf_op jit(solution)/shard_map/dot_general | solution.py:59
  531.2 43.0 %multiply_convert_fusion = (bf16[3584,2048]{1,0:T(8,128)(2,1)}, bf16[3584,2048]{1,0:T(8,128)(2,1)}) fusion(f32[3584,2048]{1,0:T(8,128)} %convert_divide_fusion.1, f32[3584,2048]{1,0:T(8,128)} %convert_divide_fusion.3, f32[3584,2048]{1,0:T(8,128)} %convert_divide_fusion.2, bf16[3584,2048]{1,0:T(8,128)(2,1)} %param.13, bf16[768,2048]{1,0:T(8,128)(2,1)S(1)} %copy-done, ...), kind=kOutput, calls=%fused_computation.4 | convolution fusion | flops 1937768448 | bytes 133562368 | tf_op jit(solution)/shard_map/dot_general | solution.py:59
  574.1 15.6 %fusion.33 = f32[256]{0:T(256)S(1)} fusion(bf16[3584,2048]{1,0:T(8,128)(2,1)} %get-tuple-element.3, bf16[768,3584]{1,0:T(8,128)(2,1)} %all-gather.7.cloned.1.call-done, bf16[768,2048]{1,0:T(8,128)(2,1)S(1)} %copy-done), kind=kOutput, calls=%fused_computation.28 | convolution fusion | flops 3760848640 | bytes 17564672 | tf_op jit(solution)/shard_map/dot_general | solution.py:64
  589.8 12.6 %fusion.30 = f32[256]{0:T(256)S(1)} fusion(f32[3584,2048]{1,0:T(8,128)} %convert_divide_fusion.1, bf16[768,3584]{1,0:T(8,128)(2,1)} %all-gather.7.cloned.1.call-done, bf16[768,2048]{1,0:T(8,128)(2,1)S(1)} %copy-done), kind=kOutput, calls=%fused_computation.27 | convolution fusion | flops 3768188672 | bytes 32244736 | tf_op jit(solution)/shard_map/dot_general | solution.py:64
  602.7 12.4 %fusion.27 = f32[256]{0:T(256)S(1)} fusion(f32[3584,2048]{1,0:T(8,128)} %convert_divide_fusion.2, bf16[768,3584]{1,0:T(8,128)(2,1)} %all-gather.7.cloned.1.call-done, bf16[768,2048]{1,0:T(8,128)(2,1)S(1)} %copy-done), kind=kOutput, calls=%fused_computation.26 | convolution fusion | flops 3768188672 | bytes 32244736 | tf_op jit(solution)/shard_map/dot_general | solution.py:64
  615.4 12.4 %fusion.24 = f32[256]{0:T(256)S(1)} fusion(f32[3584,2048]{1,0:T(8,128)} %convert_divide_fusion.3, bf16[768,3584]{1,0:T(8,128)(2,1)} %all-gather.7.cloned.1.call-done, bf16[768,2048]{1,0:T(8,128)(2,1)S(1)} %copy-done), kind=kOutput, calls=%fused_computation.25 | convolution fusion | flops 3768188672 | bytes 32244736 | tf_op jit(solution)/shard_map/dot_general | solution.py:64
  628.1 38.6 %psum.7 = f32[4,32]{1,0:T(4,128)S(1)} all-reduce(f32[4,32]{1,0:T(4,128)S(1)} %pad_maximum_fusion), channel_id=1, replica_groups=mesh['out'=8,'in'=4] {'out','in'}, use_global_device_ids=true, to_apply=%region_10.0 | all-reduce | flops 128 | bytes 1024 | tf_op jit(solution)/shard_map/psum | solution.py:73
  666.7 0.7 multiply_divide_fusion
  (34 shorter events, 1.4 us)
Async XLA Ops:
  7.2 33.1 %all-gather.9.cloned.1.call-start = ((), (), s32[]{:S(2)}) async-start(), calls=%async_computation.5 | async-start | bytes 1310720 | tf_op jit(solution)/shard_map/all_gather | solution.py:28
  7.9 83.7 %all-gather.5.cloned.1.call-start = ((), (), s32[]{:S(2)}) async-start(), calls=%async_computation.2 | async-start | bytes 8257536 | tf_op jit(solution)/shard_map/all_gather | solution.py:27
  8.6 148.1 %reduce-scatter.5.cloned.1.call-start = ((), (), s32[]{:S(2)}) async-start(), calls=%async_computation.6 | async-start | bytes 7077888 | tf_op jit(solution)/shard_map/reduce_scatter | solution.py:40
  49.0 297.1 %reduce-scatter.3.cloned.1.call-start = ((), (), s32[]{:S(2)}) async-start(), calls=%async_computation.3 | async-start | bytes 13762560 | tf_op jit(solution)/shard_map/reduce_scatter | solution.py:32
  139.9 209.3 %copy-start.2 = (s32[4,8]{1,0:T(4,128)S(1)}, s32[4,8]{1,0:T(4,128)}, u32[]{:S(2)}) copy-start(s32[4,8]{1,0:T(4,128)} %param.17) | copy-start | bytes 388
  139.9 209.4 %copy-start.4 = (s32[32]{0:T(128)S(1)}, s32[32]{0:T(128)}, u32[]{:S(2)}) copy-start(s32[32]{0:T(128)} %param.16) | copy-start | bytes 388
  139.9 241.6 %all-gather.11.cloned.1.call-start = ((), (), s32[]{:S(2)}) async-start(), calls=%async_computation.7 | async-start | bytes 3538944 | tf_op jit(solution)/shard_map/all_gather | solution.py:46
  158.7 327.3 %all-gather.7.cloned.1.call-start = ((), (), s32[]{:S(2)}) async-start(), calls=%async_computation.4 | async-start | bytes 6881280 | tf_op jit(solution)/shard_map/all_gather | solution.py:38
  381.5 120.1 %copy-start = (bf16[768,2048]{1,0:T(8,128)(2,1)S(1)}, bf16[768,2048]{1,0:T(8,128)(2,1)}, u32[]{:S(2)}) copy-start(bf16[768,2048]{1,0:T(8,128)(2,1)} %all-gather.11.cloned.1.call-done) | copy-start | bytes 9437188
  486.0 15.6 %copy-start.1 = (bf16[768,3584]{1,0:T(8,128)(2,1)S(1)}, bf16[768,3584]{1,0:T(8,128)(2,1)}, u32[]{:S(2)}) copy-start(bf16[768,3584]{1,0:T(8,128)(2,1)} %all-gather.7.cloned.1.call-done) | copy-start | bytes 16515076
  615.4 51.3 %copy-start.3 = (f32[4,32]{1,0:T(4,128)S(1)}, f32[4,32]{1,0:T(4,128)}, u32[]{:S(2)}) copy-start(f32[4,32]{1,0:T(4,128)} %multiply_reduce_fusion) | copy-start | bytes 1540
  615.4 51.3 %copy-start.5 = (f32[4]{0:T(128)S(1)}, f32[4]{0:T(128)}, u32[]{:S(2)}) copy-start(f32[4]{0:T(128)} %broadcast_multiply_fusion) | copy-start | bytes 52
Sparse Core Ops, SparseCore 0:
  9.6 30.6 all-gather.8
  42.1 49.4 all-gather.4
  95.0 61.7 reduce-scatter.4
  159.7 186.4 reduce-scatter.2
  348.1 33.4 all-gather.10
  383.6 102.3 all-gather.6
where the time goes:
time: 674 us
  waiting for transfers between devices  415 us (62%)
  matrix products  198 us (29%)
  blocking collectives  38.6 us (6%)
  between operations  14.2 us (2%)
  other arithmetic  7.45 us (1%)
    reduce_scatter x1, waiting for transfers between devices, on_device(): lax.psum_scatter(jnp.dot(picked_rows, basis_out, preferred_element_type=j...  187 us
    all_gather x1, waiting for transfers between devices, on_device(): lax.all_gather(grad_part.astype(jnp.bfloat16), 'in', axis=0, tiled=True)  104 us
    dot_general x4, matrix products, on_device(): lax.dot_general(grad_block, act_block, (((0,), (0,)), ((), ())), preferre...  88.1 us
    dot_general x4, matrix products, on_device(): lax.dot_general(rot_qin, precond.astype(jnp.bfloat16), (((1,), (1,)), (()...  53.1 us
    dot_general x1, matrix products, on_device(): jnp.dot(picked_rows, basis_out, preferred_element_type=jnp.float32)  48.3 us
    all_gather x1, waiting for transfers between devices, on_device(): grad_rows = lax.all_gather(out_grad, 'out', axis=0, tiled=True)  42.5 us
    psum x1, blocking collectives, on_device(): score = lax.psum(local_scores, ('out', 'in'))  38.6 us
    all_gather x1, waiting for transfers between devices, on_device(): act_rows = lax.all_gather(activations, 'in', axis=0, tiled=True)  31.5 us
  transfers between devices with their start and end apart: 6, of which 6 were waited for; matrix products, arithmetic and copies ran while one was open for 9% of the time, Pallas kernels for 0%

commit v1 on v0

v1 whole, which is shorter than its diff:
```python
import functools
import math

import jax
import jax.numpy as jnp
from jax import lax
from jax.experimental import pallas as pl
from jax.experimental.pallas import tpu as pltpu
from jax.sharding import PartitionSpec as P

SEQS = 4
RANK = 8
DOMAINS = 8
LAG = 2
F32 = jnp.float32
BF16 = jnp.bfloat16
ANY = pl.BlockSpec(memory_space=pl.ANY)
SMEM = pl.BlockSpec(memory_space=pltpu.SMEM)
MIB = 1024 * 1024


def swap(x, axis, size, bit):
    return lax.ppermute(x, axis, [(i, i ^ bit) for i in range(size)])


def tile_of(width, most):
    best = 128
    for tile in range(128, most + 1, 128):
        if width % tile == 0:
            best = tile
    return best


def cost(flops, moved):
    return pl.CostEstimate(flops=flops, bytes_accessed=moved, transcendentals=0)


class Order:
    def __init__(self):
        self.last = []

    def call(self, body, operands, specs, out_specs, out_shape, room=48, **options):
        count, extra, outs = len(operands), len(self.last), len(out_shape)

        def wrapped(*refs):
            ends = refs[count + extra :]
            body(*refs[:count], *ends[:outs], *ends[outs + 1 :])
            ends[outs][...] = jnp.zeros_like(ends[outs])

        *results, mark = pl.pallas_call(
            wrapped,
            in_specs=specs + [ANY] * extra,
            out_specs=list(out_specs) + [pl.BlockSpec((8, 128), lambda i: (0, 0))],
            out_shape=list(out_shape) + [jax.ShapeDtypeStruct((8, 128), F32)],
            compiler_params=pltpu.CompilerParams(vmem_limit_bytes=room * MIB),
            **options,
        )(*operands, *self.last)
        self.last = [mark]
        return results


def rotate_down(order, rows, basis, unit, first, count):
    height, depth = rows.shape
    blocks = basis.shape[1] // unit

    def body(rows_ref, basis_ref, out_ref):
        real = first + pl.program_id(0) < blocks

        @pl.when(real)
        def _():
            out_ref[...] = jnp.dot(
                rows_ref[...], basis_ref[...], preferred_element_type=F32
            ).astype(BF16)

        @pl.when(jnp.logical_not(real))
        def _():
            out_ref[...] = jnp.zeros_like(out_ref)

    return order.call(
        body,
        [rows, basis],
        [
            pl.BlockSpec((height, depth), lambda i: (0, 0), pipeline_mode=pl.Buffered(1)),
            pl.BlockSpec((depth, unit), lambda i: (0, jnp.minimum(first + i, blocks - 1))),
        ],
        grid=(count,),
        out_specs=[pl.BlockSpec((height, unit), lambda i: (i, 0))],
        out_shape=[jax.ShapeDtypeStruct((height * count, unit), BF16)],
        cost_estimate=cost(2 * height * depth * unit * count, 2 * depth * unit * count),
    )[0]


def rotate_pieces(order, pieces, offsets, tokens, basis, lower, width, most):
    depth = basis.shape[0]
    tile = tile_of(math.gcd(width, lower) if lower else width, most)
    first = lower // tile
    count = len(pieces)

    def body(offsets_ref, *refs):
        held, (basis_ref, out_ref, rows_ref, sems) = refs[:count], refs[count:]

        @pl.when(pl.program_id(0) == 0)
        def _():
            copies = []
            for n, piece in enumerate(held):
                size = piece.shape[0]
                where = pl.multiple_of(offsets_ref[n] * size, size)
                copies.append(
                    pltpu.make_async_copy(piece, rows_ref.at[pl.ds(where, size), :], sems.at[n])
                )
            for copy in copies:
                copy.start()
            for copy in copies:
                copy.wait()

        out_ref[...] = jnp.dot(rows_ref[...], basis_ref[...], preferred_element_type=F32).astype(
            BF16
        )

    return order.call(
        body,
        [offsets, *pieces, basis],
        [SMEM] + [ANY] * count + [pl.BlockSpec((depth, tile), lambda i: (0, first + i))],
        grid=(width // tile,),
        out_specs=[pl.BlockSpec((tokens, tile), lambda i: (0, i))],
        out_shape=[jax.ShapeDtypeStruct((tokens, width), BF16)],
        scratch_shapes=[
            pltpu.VMEM((tokens, depth), BF16),
            pltpu.SemaphoreType.DMA((count,)),
        ],
        cost_estimate=cost(2 * tokens * depth * width, 2 * depth * width),
    )[0]


def pick(place, groups):
    result = groups[0][1]
    for places, value in groups[1:]:
        here = functools.reduce(jnp.logical_or, [place == p for p in places])
        result = jnp.where(here, value, result)
    return result


class Line:
    def __init__(self, axis, size, place, shape, count):
        self.axis, self.size, self.place = axis, size, place
        self.shape, self.count = shape, count
        self.parts = []
        self.got = [{}, {}]

    def step(self, order, s):
        size, (rows, columns) = self.size, self.shape
        halves = 2
        block = (rows // halves, columns)
        plan, operands, specs = [], [self.place], [SMEM]
        for parity in (0, 1):
            groups = {}
            for place in range(size):
                if parity == 1 and place in (0, size - 1):
                    continue
                chunk = s - LAG * (place if place % 2 == parity else size - 1 - place)
                if 0 <= chunk < self.count:
                    groups.setdefault(chunk, []).append(place)
            if not groups:
                continue
            for chunk in groups:
                array, row, column = self.parts[chunk]
                operands.append(array)
                specs.append(
                    pl.BlockSpec(block, lambda i, r=row, c=column: (r * halves + i, c))
                )
            before = self.got[1 - parity].get(s - LAG)
            if before is not None:
                operands.append(before)
                specs.append(pl.BlockSpec(block, lambda i: (i, 0)))
            plan.append((parity, list(groups.values()), before is not None))
        outs = len(plan)

        def body(place_ref, *refs):
            place = place_ref[0]
            loads, refs = refs[len(refs) - outs :], iter(refs)
            for (_, groups, more), load in zip(plan, loads):
                value = pick(place, [(places, next(refs)[...]) for places in groups])
                if more:
                    value = (value.astype(F32) + next(refs)[...].astype(F32)).astype(BF16)
                load[...] = value

        loads = order.call(
            body,
            operands,
            specs,
            grid=(halves,),
            out_specs=[pl.BlockSpec(block, lambda i: (i, 0))] * outs,
            out_shape=[jax.ShapeDtypeStruct(self.shape, BF16)] * outs,
            cost_estimate=cost(rows * columns * 4, 2 * rows * columns * (len(operands) + outs)),
        )
        for (parity, _, _), load in zip(plan, loads):
            pairs = []
            for place in range(parity, size - 1, 2):
                pairs += [(place, place + 1), (place + 1, place)]
            self.got[parity][s] = lax.ppermute(load, self.axis, pairs)

    def terms(self, chunk):
        groups = {}
        for place in range(self.size):
            keys = []
            if place > 0:
                keys.append(((place - 1) % 2, place - 1))
            if place < self.size - 1:
                keys.append((place % 2, self.size - 2 - place))
            groups.setdefault(tuple(sorted(keys)), []).append(place)
        return [
            (places, [self.got[parity][chunk + LAG * late] for parity, late in keys])
            for keys, places in groups.items()
        ]


def score(order, line, chunk, query_chunk, query_row, act, qin_turned, eigen, mixed, first, queries):
    tokens, inner = act.shape
    unit = line.shape[1]
    tile = tile_of(unit, 256)
    tiles = unit // tile
    step = tile_of(inner, 256)
    length = tokens // SEQS
    gain = 1.0 / math.sqrt(tokens)
    operands, specs, plan = [line.place], [SMEM], []
    share = line.shape[0] // queries
    for number, row, height in ((chunk, 0, tokens), (query_chunk, query_row, queries)):
        array, low, column = line.parts[number]
        low = low * (share if height == queries else 1) + row
        operands.append(array)
        specs.append(
            pl.BlockSpec((height, tile), lambda i, r=low, c=column: (r, c * tiles + i))
        )
        groups = []
        for places, arrays in line.terms(number):
            for array in arrays:
                operands.append(array)
                specs.append(pl.BlockSpec((height, tile), lambda i, r=row: (r, i)))
            groups.append((places, len(arrays)))
        plan.append(groups)
    operands += [act, qin_turned, eigen]
    specs += [
        pl.BlockSpec((tokens, inner), lambda i: (0, 0)),
        pl.BlockSpec((inner, queries), lambda i: (0, 0)),
        pl.BlockSpec((tile, inner), lambda i: (first * tiles + i, 0)),
    ]
    aliases = {}
    if mixed is not None:
        aliases = {len(operands): 0}
        operands.append(mixed)
        specs.append(ANY)

    def body(place_ref, *refs):
        place = place_ref[0]
        mixed_ref, score_ref, half_ref = refs[-3:]
        refs = iter(refs)
        totals = []
        for groups in plan:
            own = next(refs)[...].astype(F32)
            sums = []
            for places, number in groups:
                values = [next(refs)[...].astype(F32) for _ in range(number)]
                sums.append((places, functools.reduce(jnp.add, values)))
            totals.append((own + pick(place, sums)).astype(BF16))
        act_ref, qin_ref, eigen_ref = next(refs), next(refs), next(refs)
        turned = jnp.transpose(totals[0])
        for lower in range(0, inner, step):
            span = slice(lower, lower + step)
            inverse = 1.0 / eigen_ref[:, span].astype(F32)
            total = None
            for s in range(SEQS):
                rows = slice(s * length, (s + 1) * length)
                grad = jnp.dot(turned[:, rows], act_ref[rows, span], preferred_element_type=F32)
                precond = grad * inverse
                total = precond if total is None else total + precond
                half_ref[s * tile : (s + 1) * tile, span] = precond.astype(BF16)
            mixed_ref[:, span] = (total * gain).astype(BF16)
        projected = jnp.dot(half_ref[...], qin_ref[...], preferred_element_type=F32)
        qout = jnp.transpose(totals[1]).astype(F32)

        @pl.when(pl.program_id(0) == 0)
        def _():
            score_ref[...] = jnp.zeros_like(score_ref)

        for s in range(SEQS):
            part = projected[s * tile : (s + 1) * tile] * qout
            score_ref[s : s + 1, :] += jnp.sum(part, axis=0, keepdims=True)

    return order.call(
        body,
        operands,
        specs,
        grid=(tiles,),
        out_specs=[
            pl.BlockSpec((tile, inner), lambda i: (first * tiles + i, 0)),
            pl.BlockSpec((SEQS, queries), lambda i: (0, 0)),
        ],
        out_shape=[
            jax.ShapeDtypeStruct(eigen.shape, BF16),
            jax.ShapeDtypeStruct((SEQS, queries), F32),
        ],
        scratch_shapes=[pltpu.VMEM((SEQS * tile, inner), BF16)],
        input_output_aliases=aliases,
        cost_estimate=cost(
            2 * unit * inner * (tokens * 2 + SEQS * queries), 4 * unit * inner
        ),
    )


class Gather:
    def __init__(self, own, outs):
        self.own, self.outs = own, outs
        self.index = lax.axis_index("out")
        self.bits = []
        bit = 2
        while bit < outs:
            self.bits.append(bit)
            bit *= 2
        low, high = self.bits[:2]
        self.near = [swap(own, "out", outs, low), swap(own, "out", outs, high)]
        self.pieces = [(own, self.index), self.moved((own, self.index), 1)]

    def moved(self, piece, bit):
        x, offset = piece
        rows = self.own.shape[0]
        return swap(x, "out", self.outs, bit), offset ^ (bit * (rows // x.shape[0]))

    def spread(self, order):
        rows, depth = self.own.shape
        half = rows // 2
        low, high = self.bits[:2]
        one, two = self.near

        def body(one_ref, two_ref, below_ref, above_ref):
            below_ref[...] = one_ref[...]
            above_ref[...] = two_ref[...]

        below, above = order.call(
            body,
            [one, two],
            [
                pl.BlockSpec((half, depth), lambda i: (1, 0)),
                pl.BlockSpec((half, depth), lambda i: (0, 0)),
            ],
            grid=(1,),
            out_specs=[pl.BlockSpec((half, depth), lambda i: (0, 0))] * 2,
            out_shape=[jax.ShapeDtypeStruct((half, depth), BF16)] * 2,
            cost_estimate=cost(half * depth, 8 * half * depth),
        )
        far = (self.index ^ (low | high)) * 2
        late = [
            (one, self.index ^ low),
            (two, self.index ^ high),
            (swap(above, "out", self.outs, low), far),
            (swap(below, "out", self.outs, high), far + 1),
        ]
        self.pieces += late + [self.moved(piece, 1) for piece in late]
        for bit in self.bits[2:]:
            self.pieces += [self.moved(piece, bit) for piece in self.pieces]
        offsets = jnp.stack([offset for _, offset in self.pieces]).astype(jnp.int32)
        return [x for x, _ in self.pieces], offsets


class SumOut:
    def __init__(self, outs, core):
        self.outs, self.core = outs, core
        self.bits = []
        bit = 2
        while bit < outs:
            self.bits.append(bit)
            bit *= 2

    def start(self, order, rows, more, basis, tile):
        (tokens, depth), extra = rows.shape, more.shape[0]
        half = (tokens + extra) // 2
        width = basis.shape[1]

        def body(core_ref, rows_ref, more_ref, basis_ref, keep_ref, give_ref, all_ref):
            @pl.when(pl.program_id(0) == 0)
            def _():
                all_ref[:tokens] = rows_ref[...]
                all_ref[tokens:] = more_ref[...]

            for ref, side in ((keep_ref, core_ref[0]), (give_ref, 1 - core_ref[0])):
                at = pl.multiple_of(side * half, half)
                ref[...] = jnp.dot(
                    all_ref[pl.ds(at, half), :], basis_ref[...], preferred_element_type=F32
                ).astype(ref.dtype)

        self.keep, give = order.call(
            body,
            [self.core, rows, more, basis],
            [
                SMEM,
                pl.BlockSpec((tokens, depth), lambda i: (0, 0)),
                pl.BlockSpec((extra, depth), lambda i: (0, 0)),
                pl.BlockSpec((depth, tile), lambda i: (0, i)),
            ],
            grid=(width // tile,),
            out_specs=[pl.BlockSpec((half, tile), lambda i: (0, i))] * 2,
            out_shape=[
                jax.ShapeDtypeStruct((half, width), F32),
                jax.ShapeDtypeStruct((half, width), BF16),
            ],
            scratch_shapes=[pltpu.VMEM((tokens + extra, depth), BF16)],
            cost_estimate=cost(4 * half * depth * width, 2 * depth * width),
        )
        self.got = swap(give, "out", self.outs, 1)
        self.stage, self.done = 0, False

    def pieces(self):
        half = self.keep.shape[0]
        return half // 2, self.keep.shape[1]

    def advance(self, order):
        piece, width = self.pieces()
        grid = 2
        block = (piece // grid, width)
        done = self.stage == len(self.bits)
        if self.stage == 0:
            operands = [self.keep, self.keep, self.got, self.got]
            specs = [pl.BlockSpec(block, lambda i, n=n: (n * grid + i, 0)) for n in (0, 1, 0, 1)]
        else:
            operands = list(self.held) + list(self.got)
            specs = [pl.BlockSpec(block, lambda i: (i, 0))] * 4

        def body(low, high, low_more, high_more, *outs):
            for n, (a, b) in enumerate(((low, low_more), (high, high_more))):
                value = a[...] + b[...].astype(F32)
                if done:
                    outs[0][n] = value.astype(BF16)
                else:
                    outs[n][...] = value.astype(BF16)
                    outs[2 + n][...] = value

        if done:
            out_specs = [pl.BlockSpec((2,) + block, lambda i: (0, i, 0))]
            out_shape = [jax.ShapeDtypeStruct((2, piece, width), BF16)]
        else:
            out_specs = [pl.BlockSpec(block, lambda i: (i, 0))] * 4
            out_shape = [
                jax.ShapeDtypeStruct((piece, width), kind) for kind in (BF16, BF16, F32, F32)
            ]
        outs = order.call(
            body,
            operands,
            specs,
            grid=(grid,),
            out_specs=out_specs,
            out_shape=out_shape,
            cost_estimate=cost(2 * piece * width, 12 * piece * width),
        )
        if done:
            self.mine = outs[0].reshape(2 * piece, width)
            self.other = swap(self.mine, "out", self.outs, 1)
            self.done = True
            return
        self.held = outs[2:]
        self.got = [
            swap(outs[0], "out", self.outs, self.bits[self.stage]),
            swap(outs[1], "out", self.outs, self.bits[-1 - self.stage]),
        ]
        self.stage += 1

    def finish(self, order, tokens):
        half, width = self.mine.shape
        extra = 2 * half - tokens

        def body(core_ref, mine_ref, other_ref, act_ref, turned_ref):
            first = core_ref[0] == 0
            top = jnp.where(first, mine_ref[...], other_ref[...])
            bottom = jnp.where(first, other_ref[...], mine_ref[...])
            act_ref[:half] = top
            act_ref[half:] = bottom[: tokens - half]
            turned_ref[...] = jnp.transpose(bottom[tokens - half :])

        tile = tile_of(width, 512)
        return order.call(
            body,
            [self.core, self.mine, self.other],
            [SMEM] + [pl.BlockSpec((half, tile), lambda i: (0, i))] * 2,
            grid=(width // tile,),
            out_specs=[
                pl.BlockSpec((tokens, tile), lambda i: (0, i)),
                pl.BlockSpec((tile, extra), lambda i: (i, 0)),
            ],
            out_shape=[
                jax.ShapeDtypeStruct((tokens, width), BF16),
                jax.ShapeDtypeStruct((width, extra), BF16),
            ],
            cost_estimate=cost(2 * half * width, 8 * half * width),
        )


def on_device(
    outs,
    ins,
    activations,
    out_grad,
    basis_out,
    basis_in,
    eigenvalues,
    query_out,
    query_in,
    query_domain,
    seq_weight,
):
    tokens = activations.shape[0] * ins
    queries = query_out.shape[0]
    columns = basis_out.shape[1]
    inner = basis_in.shape[1]
    order = Order()

    act_rows = lax.all_gather(activations, "in", axis=0, tiled=True)
    gather = Gather(out_grad, outs)
    core = (lax.axis_index("out") & 1).astype(jnp.int32).reshape(1)

    unit = tile_of(columns, 512)
    spans = columns // unit
    share = tokens // queries
    ahead = -(-spans // share)
    place = lax.axis_index("in").astype(jnp.int32).reshape(1)
    line = Line("in", ins, place, (tokens, unit), ahead + spans)

    def queries_part(first, count):
        part = rotate_down(order, query_out, basis_out, unit, first * share, count * share)
        line.parts += [(part, c, 0) for c in range(count)]

    def grads_part(first, count):
        part = rotate_pieces(
            order, *gathered, tokens, basis_out, first * unit, count * unit, 256
        )
        line.parts += [(part, 0, c) for c in range(count)]

    mixed, scores = None, []

    def score_part(g):
        nonlocal mixed
        mixed, part = score(
            order,
            line,
            ahead + g,
            g // share,
            g % share,
            rot_act,
            qin_turned,
            eigenvalues,
            mixed,
            g,
            queries,
        )
        scores.append(part)

    late = LAG * (ins - 2)
    last = ahead + spans - 1 + late
    gathered = rot_act = qin_turned = None
    total = SumOut(outs, core)
    plan = {2: 2, 4: 2, 6: spans}
    made = 0
    for s in range(last + 1):
        if s == 0:
            queries_part(0, 1)
        elif made < spans and s >= ahead + made:
            grads_part(made, 1)
            made += 1
        line.step(order, s)
        target = s - 1 - late - ahead
        if s == 0 and ahead > 1:
            queries_part(1, ahead - 1)
        elif s == 1:
            gathered = gather.spread(order)
        elif s == 2:
            total.start(order, act_rows, query_in, basis_in, tile_of(inner, 512))
        while rot_act is None and s >= 3 and (s % 2 == 1 or s > 7 or target >= 0):
            if not total.done:
                total.advance(order)
            else:
                rot_act, qin_turned = total.finish(order, tokens)
            if target < 0:
                break
        count = min(plan.get(s, 0), spans - made)
        if count > 0:
            grads_part(made, count)
            made += count
        if 0 <= target < spans:
            score_part(target)
    while len(scores) < spans:
        score_part(len(scores))

    scores = functools.reduce(jnp.add, scores)
    for axis, size in (("out", outs), ("in", ins)):
        bit = 1
        while bit < size:
            scores = scores + swap(scores, axis, size, bit)
            bit *= 2
    summed = jnp.sum(scores.reshape(SEQS, queries // RANK, RANK), axis=2)
    weights = seq_weight.astype(F32)
    onehot = (query_domain[:, None] == jnp.arange(DOMAINS, dtype=jnp.int32)[None, :]).astype(F32)
    picked = jnp.sum(weights[:, None, :] * onehot[None, :, :], axis=2)
    mean_weight = jnp.sum(weights, axis=1, keepdims=True) / DOMAINS
    return (mixed, summed * picked / mean_weight)


def solution(mesh):
    return jax.shard_map(
        functools.partial(on_device, mesh.shape["out"], mesh.shape["in"]),
        mesh=mesh,
        in_specs=(
            P("in", "out"),
            P("out", "in"),
            P("in", "out"),
            P("out", "in"),
            P("out", "in"),
            P(None, "in"),
            P(None, "out"),
            P(),
            P(),
        ),
        out_specs=(P("out", "in"), P()),
        check_vma=False,
    )
```

time: 674 us -> 293 us (0.43)
  waiting for transfers between devices: 415 us -> 43.4 us
  matrix products: 198 us -> 0 us
  Pallas kernels: 0 us -> 154 us
  starting transfers between devices: 0.42 us -> 57.7 us
  blocking collectives: 38.6 us -> 0 us
  local copies, waits for them, and re-layouts: 0.35 us -> 20.6 us
    reduce_scatter x2 -> x0, waiting for transfers between devices: 204 us -> none  [the longest x1 187 us: on_device(): lax.psum_scatter(jnp.dot(picked_rows, basis_out, preferred_element_type=j...]
    dot_general x10 -> x0, matrix products: 198 us -> none  [the longest x4 88.1 us: on_device(): lax.dot_general(grad_block, act_block, (((0,), (0,)), ((), ())), preferre...]
    all_gather x3 -> x0, waiting for transfers between devices: 178 us -> none  [the longest x1 104 us: on_device(): lax.all_gather(grad_part.astype(jnp.bfloat16), 'in', axis=0, tiled=True)]
    pallas_call x0 -> x33, Pallas kernels: none -> 154 us  [call(): pl.pallas_call(wrapped, in_specs=specs + [ANY] * extra, out_specs=list(ou...]
    ppermute x0 -> x46, starting transfers between devices: none -> 57.6 us  [the longest x26 41 us: step(): self.got[parity][s] = lax.ppermute(load, self.axis, pairs)]
    ppermute x0 -> x46, waiting for transfers between devices: none -> 43.3 us  [the longest x26 30.9 us: step(): self.got[parity][s] = lax.ppermute(load, self.axis, pairs)]
    psum x1 -> x0, blocking collectives: 38.6 us -> none  [on_device(): score = lax.psum(local_scores, ('out', 'in'))]
    all_gather x1, waiting for transfers between devices: 31.5 us -> 0.01 us  [on_device(): act_rows = lax.all_gather(activations, 'in', axis=0, tiled=True)]
  transfers between devices with their start and end apart: 6 -> 47, of which waited for: 6 -> 11; matrix products, arithmetic and copies ran while one was open for 9% -> 0% of each run, Pallas kernels for 0% -> 49%
where the time goes in v1:
time: 293 us; the launch traced here: 291 us
  Pallas kernels  154 us (53%)
  starting transfers between devices  57.7 us (20%)
  waiting for transfers between devices  43.4 us (15%)
  local copies, waits for them, and re-layouts  20.6 us (7%)
  between operations  14.7 us (5%)
    pallas_call x33, Pallas kernels, call(): pl.pallas_call(wrapped, in_specs=specs + [ANY] * extra, out_specs=list(ou...  154 us
    ppermute x26, starting transfers between devices, step(): self.got[parity][s] = lax.ppermute(load, self.axis, pairs)  41 us
    ppermute x26, waiting for transfers between devices, step(): self.got[parity][s] = lax.ppermute(load, self.axis, pairs)  30.9 us
    unnamed x86, local copies, waits for them, and re-layouts  20.4 us
    ppermute x20, starting transfers between devices, swap(): return lax.ppermute(x, axis, [(i, i ^ bit) for i in range(size)])  16.6 us
    ppermute x20, waiting for transfers between devices, swap(): return lax.ppermute(x, axis, [(i, i ^ bit) for i in range(size)])  12.4 us
  transfers between devices with their start and end apart: 47, of which 11 were waited for; matrix products, arithmetic and copies ran while one was open for 0% of the time, Pallas kernels for 49%

profile of v1, /device:TPU:0, one launch (start us, length us, event | category | flops | bytes accessed | tf_op | source)
XLA Modules:
  0.0 291.3 jit_solution(3367659822163215611)
XLA Ops:
  13.9 7.3 %shard_map.104 = (bf16[512,512]{1,0:T(8,128)(2,1)S(1)}, f32[8,128]{1,0:T(8,128)S(1)}) custom-call(bf16[256,7168]{1,0:T(8,128)(2,1)S(1)} %copy-done.4, bf16[7168,3584]{1,0:T(8,128)(2,1)} %refs_11_.12), custom_call_target="tpu_custom_call" | custom-call | flops 3758096384 | bytes 14680064 | tf_op jit(solution)/shard_map/pallas_call | solution.py:50
  25.0 15.7 %shard_map.106 = (bf16[1536,512]{1,0:T(8,128)(2,1)S(1)}, f32[8,128]{1,0:T(8,128)S(1)}) custom-call(bf16[256,7168]{1,0:T(8,128)(2,1)S(1)} %copy-done.5, bf16[7168,3584]{1,0:T(8,128)(2,1)} %refs_11_.12, f32[8,128]{1,0:T(8,128)S(1)} %get-tuple-element.96.refs_2_), custom_call_target="tpu_custom_call" | custom-call | flops 11274289152 | bytes 44040192 | tf_op jit(solution)/shard_map/pallas_call | solution.py:50
  43.0 7.5 %collective-permute-done.9.refs_3_.refs_7_ = bf16[512,512]{1,0:T(8,128)(2,1)S(1)} collective-permute-done((bf16[512,512]{1,0:T(8,128)(2,1)S(1)}, bf16[512,512]{1,0:T(8,128)(2,1)S(1)}, u32[]{:S(2)}, u32[]{:S(2)}) %collective-permute-start.9) | collective-permute-done | bytes 524320 | tf_op jit(solution)/shard_map/ppermute | solution.py:200
  58.1 6.5 %shard_map.110 = (f32[384,2048]{1,0:T(8,128)}, bf16[384,2048]{1,0:T(8,128)(2,1)}, f32[8,128]{1,0:T(8,128)S(1)}) custom-call(s32[1]{0:T(128)} %bitcast.11.refs_0_, bf16[512,1024]{1,0:T(8,128)(2,1)S(1)} %copy-done.32, bf16[256,1024]{1,0:T(8,128)(2,1)S(1)} %copy-done.33, bf16[1024,2048]{1,0:T(8,128)(2,1)} %refs_3_.1, f32[8,128]{1,0:T(8,128)S(1)} %get-tuple-element.104.refs_4_), custom_call_target="tpu_custom_call" | custom-call | flops 3221225472 | bytes 4194304 | tf_op jit(solution)/shard_map/pallas_call | solution.py:50
  66.0 4.8 %collective-permute-start.11 = (bf16[512,512]{1,0:T(8,128)(2,1)}, bf16[512,512]{1,0:T(8,128)(2,1)S(1)}, u32[]{:S(2)}, u32[]{:S(2)}) collective-permute-start(bf16[512,512]{1,0:T(8,128)(2,1)} %copy-done.35), channel_id=1, source_target_pairs={{0,1},{1,0},{2,3},{3,2},{4,5},{5,4},{6,7},{7,6},{8,9},{9,8},{10,11... | collective-permute-start | bytes 1572872 | tf_op jit(solution)/shard_map/ppermute | solution.py:200
  71.9 14.0 %shard_map.111 = (bf16[512,1024]{1,0:T(8,128)(2,1)}, f32[8,128]{1,0:T(8,128)S(1)}) custom-call(s32[10]{0:T(128)S(1)} %stack.43.refs_0_, bf16[64,7168]{1,0:T(8,128)(2,1)S(1)} %copy-done.9, bf16[64,7168]{1,0:T(8,128)(2,1)} %collective-permute-done.refs_2_, bf16[64,7168]{1,0:T(8,128)(2,1)S(1)} %collective-permute-done.1.refs_0_.refs_3_, ...), custom_call_target="tpu_custom_call" | custom-call | flops 7516192768 | bytes 14680064 | tf_op jit(solution)/shard_map/pallas_call | solution.py:50
  87.0 3.5 %shard_map.113 = (bf16[192,2048]{1,0:T(8,128)(2,1)}, bf16[192,2048]{1,0:T(8,128)(2,1)}, f32[192,2048]{1,0:T(8,128)S(1)}, f32[192,2048]{1,0:T(8,128)S(1)}, f32[8,128]{1,0:T(8,128)S(1)}) custom-call(f32[384,2048]{1,0:T(8,128)} %get-tuple-element.109.refs_0_.refs_1_, f32[384,2048]{1,0:T(8,128)} %get-tuple-element.109.refs_0_.refs_1_, ...), custom_call_target="tpu_custom_call" | custom-call | flops 786432 | bytes 4718592 | tf_op jit(solution)/shard_map/pallas_call | solution.py:50
  98.8 3.3 %collective-permute-start.15 = (bf16[512,512]{1,0:T(8,128)(2,1)}, bf16[512,512]{1,0:T(8,128)(2,1)S(1)}, u32[]{:S(2)}, u32[]{:S(2)}) collective-permute-start(bf16[512,512]{1,0:T(8,128)(2,1)} %get-tuple-element.118), channel_id=1, source_target_pairs={{0,1},{1,0},{2,3},{3,2},{4,5},{5,4},{6,7},{7,6},{8,9},{9,8},{10,11... | collective-permute-start | bytes 1572872 | tf_op jit(solution)/shard_map/ppermute | solution.py:200
  102.1 14.0 %shard_map.115 = (bf16[512,1024]{1,0:T(8,128)(2,1)}, f32[8,128]{1,0:T(8,128)S(1)}) custom-call(s32[10]{0:T(128)S(1)} %stack.43.refs_0_, bf16[64,7168]{1,0:T(8,128)(2,1)S(1)} %copy-done.10, bf16[64,7168]{1,0:T(8,128)(2,1)} %collective-permute-done.refs_2_, bf16[64,7168]{1,0:T(8,128)(2,1)S(1)} %collective-permute-done.1.refs_0_.refs_3_, ...), custom_call_target="tpu_custom_call" | custom-call | flops 7516192768 | bytes 14680064 | tf_op jit(solution)/shard_map/pallas_call | solution.py:50
  120.5 3.2 %shard_map.117 = (bf16[192,2048]{1,0:T(8,128)(2,1)}, bf16[192,2048]{1,0:T(8,128)(2,1)}, f32[192,2048]{1,0:T(8,128)S(1)}, f32[192,2048]{1,0:T(8,128)}, f32[8,128]{1,0:T(8,128)S(1)}) custom-call(f32[192,2048]{1,0:T(8,128)} %copy-done.26, f32[192,2048]{1,0:T(8,128)} %copy-done.27, bf16[192,2048]{1,0:T(8,128)(2,1)S(1)} %collective-permute-done.16.refs_2_, ...), custom_call_target="tpu_custom_call" | custom-call | flops 786432 | bytes 4718592 | tf_op jit(solution)/shard_map/pallas_call | solution.py:50
  130.0 18.2 %shard_map.119 = (bf16[512,1536]{1,0:T(8,128)(2,1)}, f32[8,128]{1,0:T(8,128)S(1)}) custom-call(s32[10]{0:T(128)S(1)} %stack.43.refs_0_, bf16[64,7168]{1,0:T(8,128)(2,1)S(1)} %copy-done.10, bf16[64,7168]{1,0:T(8,128)(2,1)} %collective-permute-done.refs_2_, bf16[64,7168]{1,0:T(8,128)(2,1)S(1)} %collective-permute-done.1.refs_0_.refs_3_, ...), custom_call_target="tpu_custom_call" | custom-call | flops 11274289152 | bytes 22020096 | tf_op jit(solution)/shard_map/pallas_call | solution.py:50
  153.4 3.3 %collective-permute-start.21 = (bf16[512,512]{1,0:T(8,128)(2,1)S(1)}, bf16[512,512]{1,0:T(8,128)(2,1)S(1)}, u32[]{:S(2)}, u32[]{:S(2)}) collective-permute-start(bf16[512,512]{1,0:T(8,128)(2,1)S(1)} %copy-done.38), channel_id=1, source_target_pairs={{0,1},{1,0},{2,3},{3,2},{4,5},{5,4},{6,7},{7,6},{8,9},{9,8},{10,11... | collective-permute-start | bytes 1572872 | tf_op jit(solution)/shard_map/ppermute | solution.py:200
  159.4 9.9 %collective-permute-done.21.refs_5_.refs_3_.refs_6_ = bf16[512,512]{1,0:T(8,128)(2,1)S(1)} collective-permute-done((bf16[512,512]{1,0:T(8,128)(2,1)S(1)}, bf16[512,512]{1,0:T(8,128)(2,1)S(1)}, u32[]{:S(2)}, u32[]{:S(2)}) %collective-permute-start.21) | collective-permute-done | bytes 524320 | tf_op jit(solution)/shard_map/ppermute | solution.py:200
  175.2 3.9 %shard_map.123 = (bf16[512,2048]{1,0:T(8,128)(2,1)}, bf16[2048,256]{1,0:T(8,128)(2,1)S(1)}, f32[8,128]{1,0:T(8,128)S(1)}) custom-call(s32[1]{0:T(128)} %bitcast.11.refs_0_, bf16[384,2048]{1,0:T(8,128)(2,1)} %bitcast.12.refs_1_, bf16[384,2048]{1,0:T(8,128)(2,1)S(1)} %copy-done.31, f32[8,128]{1,0:T(8,128)S(1)} %get-tuple-element.144.refs_3_), custom_call_target="tpu_custom_call" | custom-call | flops 1572864 | bytes 6291456 | tf_op jit(solution)/shard_map/pallas_call | solution.py:50
  183.9 8.0 %collective-permute-done.27.refs_2_.refs_5_.refs_3_ = bf16[512,512]{1,0:T(8,128)(2,1)S(1)} collective-permute-done((bf16[512,512]{1,0:T(8,128)(2,1)S(1)}, bf16[512,512]{1,0:T(8,128)(2,1)S(1)}, u32[]{:S(2)}, u32[]{:S(2)}) %collective-permute-start.27) | collective-permute-done | bytes 524320 | tf_op jit(solution)/shard_map/ppermute | solution.py:200
  191.9 8.1 %shard_map.125 = (bf16[3584,2048]{1,0:T(8,128)(2,1)}, f32[4,256]{1,0:T(4,128)S(1)}, f32[8,128]{1,0:T(8,128)S(1)}) custom-call(s32[1]{0:T(128)} %bitcast.refs_0_, bf16[512,1024]{1,0:T(8,128)(2,1)S(1)} %copy-done.3, bf16[512,512]{1,0:T(8,128)(2,1)S(1)} %collective-permute-done.27.refs_2_.refs_5_.refs_3_, ...), custom_call_target="tpu_custom_call" | custom-call | flops 4294967296 | bytes 4194304 | tf_op jit(solution)/shard_map/pallas_call | solution.py:50
  203.2 8.1 %shard_map.127 = (bf16[3584,2048]{1,0:T(8,128)(2,1)}, f32[4,256]{1,0:T(4,128)S(1)}, f32[8,128]{1,0:T(8,128)S(1)}) custom-call(s32[1]{0:T(128)} %bitcast.refs_0_, bf16[512,1024]{1,0:T(8,128)(2,1)S(1)} %copy-done.3, bf16[512,512]{1,0:T(8,128)(2,1)S(1)} %collective-permute-done.33.refs_2_.refs_4_.refs_3_, ...), custom_call_target="tpu_custom_call", output_to_operand_aliasing={{0}: (12, {})} | custom-call | flops 4294967296 | bytes 4194304 | tf_op jit(solution)/shard_map/pallas_call | solution.py:50
  214.5 8.2 %shard_map.129 = (bf16[3584,2048]{1,0:T(8,128)(2,1)}, f32[4,256]{1,0:T(4,128)S(1)}, f32[8,128]{1,0:T(8,128)S(1)}) custom-call(s32[1]{0:T(128)} %bitcast.refs_0_, bf16[512,1024]{1,0:T(8,128)(2,1)S(1)} %copy-done.2, bf16[512,512]{1,0:T(8,128)(2,1)S(1)} %collective-permute-done.32.refs_2_.refs_4_.refs_3_, ...), custom_call_target="tpu_custom_call", output_to_operand_aliasing={{0}: (12, {})} | custom-call | flops 4294967296 | bytes 4194304 | tf_op jit(solution)/shard_map/pallas_call | solution.py:50
  226.6 8.2 %shard_map.131 = (bf16[3584,2048]{1,0:T(8,128)(2,1)}, f32[4,256]{1,0:T(4,128)S(1)}, f32[8,128]{1,0:T(8,128)S(1)}) custom-call(s32[1]{0:T(128)} %bitcast.refs_0_, bf16[512,1024]{1,0:T(8,128)(2,1)S(1)} %copy-done.2, bf16[512,512]{1,0:T(8,128)(2,1)S(1)} %collective-permute-done.37.refs_2_, ...), custom_call_target="tpu_custom_call", output_to_operand_aliasing={{0}: (12, {})} | custom-call | flops 4294967296 | bytes 4194304 | tf_op jit(solution)/shard_map/pallas_call | solution.py:50
  237.0 8.1 %shard_map.133 = (bf16[3584,2048]{1,0:T(8,128)(2,1)}, f32[4,256]{1,0:T(4,128)S(1)}, f32[8,128]{1,0:T(8,128)S(1)}) custom-call(s32[1]{0:T(128)} %bitcast.refs_0_, bf16[512,1536]{1,0:T(8,128)(2,1)S(1)} %copy-done.1, bf16[512,512]{1,0:T(8,128)(2,1)S(1)} %collective-permute-done.36.refs_2_, ...), custom_call_target="tpu_custom_call", output_to_operand_aliasing={{0}: (12, {})} | custom-call | flops 4294967296 | bytes 4194304 | tf_op jit(solution)/shard_map/pallas_call | solution.py:50
  249.3 8.3 %shard_map.135 = (bf16[3584,2048]{1,0:T(8,128)(2,1)}, f32[4,256]{1,0:T(4,128)S(1)}, f32[8,128]{1,0:T(8,128)S(1)}) custom-call(s32[1]{0:T(128)} %bitcast.refs_0_, bf16[512,1536]{1,0:T(8,128)(2,1)S(1)} %copy-done.1, bf16[512,512]{1,0:T(8,128)(2,1)S(1)} %collective-permute-done.40.refs_2_, ...), custom_call_target="tpu_custom_call", output_to_operand_aliasing={{0}: (12, {})} | custom-call | flops 4294967296 | bytes 4194304 | tf_op jit(solution)/shard_map/pallas_call | solution.py:50
  258.9 8.1 %shard_map.136 = (bf16[3584,2048]{1,0:T(8,128)(2,1)}, f32[4,256]{1,0:T(4,128)S(1)}, f32[8,128]{1,0:T(8,128)}) custom-call(s32[1]{0:T(128)} %bitcast.refs_0_, bf16[512,1536]{1,0:T(8,128)(2,1)S(1)} %copy-done.1, bf16[512,512]{1,0:T(8,128)(2,1)S(1)} %collective-permute-done.39.refs_2_, ...), custom_call_target="tpu_custom_call", output_to_operand_aliasing={{0}: (12, {})} | custom-call | flops 4294967296 | bytes 4194304 | tf_op jit(solution)/shard_map/pallas_call | solution.py:50
  268.3 3.6 %collective-permute-done.42 = f32[4,256]{1,0:T(4,128)S(1)} collective-permute-done((f32[4,256]{1,0:T(4,128)S(1)}, f32[4,256]{1,0:T(4,128)S(1)}, u32[]{:S(2)}, u32[]{:S(2)}) %collective-permute-start.42) | collective-permute-done | bytes 4128 | tf_op jit(solution)/shard_map/ppermute | solution.py:23
  272.1 3.4 %collective-permute-done.43 = f32[4,256]{1,0:T(4,128)S(1)} collective-permute-done((f32[4,256]{1,0:T(4,128)S(1)}, f32[4,256]{1,0:T(4,128)S(1)}, u32[]{:S(2)}, u32[]{:S(2)}) %collective-permute-start.43) | collective-permute-done | bytes 4128 | tf_op jit(solution)/shard_map/ppermute | solution.py:23
  (205 shorter events, 89.3 us)
Async XLA Ops:
  7.2 48.7 %all-gather.2.cloned.1.call-start = ((), (), s32[]{:S(2)}) async-start(), calls=%async_computation | async-start | bytes 1310720 | tf_op jit(solution)/shard_map/all_gather | solution.py:514
  7.2 57.4 %collective-permute-start = (bf16[64,7168]{1,0:T(8,128)(2,1)}, bf16[64,7168]{1,0:T(8,128)(2,1)}, u32[]{:S(2)}, u32[]{:S(2)}) collective-permute-start(bf16[64,7168]{1,0:T(8,128)(2,1)} %refs_1_.9), channel_id=1, source_target_pairs={{0,4},{4,0},{8,12},{12,8},{16,20},{20,16},{24,28},{28,24},{1,5},{5... | collective-permute-start | bytes 2752520 | tf_op jit(solution)/shard_map/ppermute | solution.py:23
  7.7 33.1 %collective-permute-start.1 = (bf16[64,7168]{1,0:T(8,128)(2,1)}, bf16[64,7168]{1,0:T(8,128)(2,1)S(1)}, u32[]{:S(2)}, u32[]{:S(2)}) collective-permute-start(bf16[64,7168]{1,0:T(8,128)(2,1)} %refs_1_.9), channel_id=1, source_target_pairs={{0,8},{4,12},{8,0},{12,4},{16,24},{20,28},{24,16},{28,20},{1,9},{5... | collective-permute-start | bytes 2752520 | tf_op jit(solution)/shard_map/ppermute | solution.py:23
  10.3 30.5 %collective-permute-start.2 = (bf16[64,7168]{1,0:T(8,128)(2,1)}, bf16[64,7168]{1,0:T(8,128)(2,1)S(1)}, u32[]{:S(2)}, u32[]{:S(2)}) collective-permute-start(bf16[64,7168]{1,0:T(8,128)(2,1)} %refs_1_.9), channel_id=1, source_target_pairs={{0,16},{4,20},{8,24},{12,28},{16,0},{20,4},{24,8},{28,12},{1,17},{... | collective-permute-start | bytes 2752520 | tf_op jit(solution)/shard_map/ppermute | solution.py:23
  21.3 29.3 %collective-permute-start.9 = (bf16[512,512]{1,0:T(8,128)(2,1)S(1)}, bf16[512,512]{1,0:T(8,128)(2,1)S(1)}, u32[]{:S(2)}, u32[]{:S(2)}) collective-permute-start(bf16[512,512]{1,0:T(8,128)(2,1)S(1)} %get-tuple-element.102), channel_id=1, source_target_pairs={{0,1},{1,0},{2,3},{3,2},{4,5},{5,4},{6,7},{7,6},{8,9},{9,8},{10,11... | collective-permute-start | bytes 1572872 | tf_op jit(solution)/shard_map/ppermute | solution.py:200
  43.0 22.1 %collective-permute-start.5 = (bf16[64,7168]{1,0:T(8,128)(2,1)S(1)}, bf16[64,7168]{1,0:T(8,128)(2,1)}, u32[]{:S(2)}, u32[]{:S(2)}) collective-permute-start(bf16[64,7168]{1,0:T(8,128)(2,1)S(1)} %collective-permute-done.1.refs_0_.refs_3_), channel_id=1, source_target_pairs={{0,4},{4,0},{8,12},{12,8},{16,20},{20,16},{24,28},{28,24},{1,5},{5... | collective-permute-start | bytes 2752520 | tf_op jit(solution)/shard_map/ppermute | solution.py:23
  64.6 22.3 %collective-permute-start.12 = (bf16[384,2048]{1,0:T(8,128)(2,1)}, bf16[384,2048]{1,0:T(8,128)(2,1)}, u32[]{:S(2)}, u32[]{:S(2)}) collective-permute-start(bf16[384,2048]{1,0:T(8,128)(2,1)} %get-tuple-element.110), channel_id=1, source_target_pairs={{0,4},{4,0},{8,12},{12,8},{16,20},{20,16},{24,28},{28,24},{1,5},{5... | collective-permute-start | bytes 4718600 | tf_op jit(solution)/shard_map/ppermute | solution.py:23
  65.3 30.4 %collective-permute-start.10 = (bf16[512,512]{1,0:T(8,128)(2,1)}, bf16[512,512]{1,0:T(8,128)(2,1)S(1)}, u32[]{:S(2)}, u32[]{:S(2)}) collective-permute-start(bf16[512,512]{1,0:T(8,128)(2,1)} %copy-done.36), channel_id=1, source_target_pairs={{1,2},{2,1},{5,6},{6,5},{9,10},{10,9},{13,14},{14,13},{17,18},{18,... | collective-permute-start | bytes 1572872 | tf_op jit(solution)/shard_map/ppermute | solution.py:200
  66.0 31.0 %collective-permute-start.11 = (bf16[512,512]{1,0:T(8,128)(2,1)}, bf16[512,512]{1,0:T(8,128)(2,1)S(1)}, u32[]{:S(2)}, u32[]{:S(2)}) collective-permute-start(bf16[512,512]{1,0:T(8,128)(2,1)} %copy-done.35), channel_id=1, source_target_pairs={{0,1},{1,0},{2,3},{3,2},{4,5},{5,4},{6,7},{7,6},{8,9},{9,8},{10,11... | collective-permute-start | bytes 1572872 | tf_op jit(solution)/shard_map/ppermute | solution.py:200
  92.8 25.6 %collective-permute-start.16 = (bf16[192,2048]{1,0:T(8,128)(2,1)}, bf16[192,2048]{1,0:T(8,128)(2,1)S(1)}, u32[]{:S(2)}, u32[]{:S(2)}) collective-permute-start(bf16[192,2048]{1,0:T(8,128)(2,1)} %get-tuple-element.121), channel_id=1, source_target_pairs={{0,8},{4,12},{8,0},{12,4},{16,24},{20,28},{24,16},{28,20},{1,9},{5... | collective-permute-start | bytes 2359304 | tf_op jit(solution)/shard_map/ppermute | solution.py:23
  94.2 26.3 %collective-permute-start.17 = (bf16[192,2048]{1,0:T(8,128)(2,1)}, bf16[192,2048]{1,0:T(8,128)(2,1)S(1)}, u32[]{:S(2)}, u32[]{:S(2)}) collective-permute-start(bf16[192,2048]{1,0:T(8,128)(2,1)} %get-tuple-element.122), channel_id=1, source_target_pairs={{0,16},{4,20},{8,24},{12,28},{16,0},{20,4},{24,8},{28,12},{1,17},{... | collective-permute-start | bytes 2359304 | tf_op jit(solution)/shard_map/ppermute | solution.py:23
  98.1 27.5 %collective-permute-start.14 = (bf16[512,512]{1,0:T(8,128)(2,1)}, bf16[512,512]{1,0:T(8,128)(2,1)S(1)}, u32[]{:S(2)}, u32[]{:S(2)}) collective-permute-start(bf16[512,512]{1,0:T(8,128)(2,1)} %get-tuple-element.117), channel_id=1, source_target_pairs={{1,2},{2,1},{5,6},{6,5},{9,10},{10,9},{13,14},{14,13},{17,18},{18,... | collective-permute-start | bytes 1572872 | tf_op jit(solution)/shard_map/ppermute | solution.py:200
  98.8 29.1 %collective-permute-start.15 = (bf16[512,512]{1,0:T(8,128)(2,1)}, bf16[512,512]{1,0:T(8,128)(2,1)S(1)}, u32[]{:S(2)}, u32[]{:S(2)}) collective-permute-start(bf16[512,512]{1,0:T(8,128)(2,1)} %get-tuple-element.118), channel_id=1, source_target_pairs={{0,1},{1,0},{2,3},{3,2},{4,5},{5,4},{6,7},{7,6},{8,9},{9,8},{10,11... | collective-permute-start | bytes 1572872 | tf_op jit(solution)/shard_map/ppermute | solution.py:200
  117.4 30.9 %collective-permute-start.24 = (bf16[512,512]{1,0:T(8,128)(2,1)}, bf16[512,512]{1,0:T(8,128)(2,1)S(1)}, u32[]{:S(2)}, u32[]{:S(2)}) collective-permute-start(bf16[512,512]{1,0:T(8,128)(2,1)} %get-tuple-element.136), channel_id=1, source_target_pairs={{1,2},{2,1},{5,6},{6,5},{9,10},{10,9},{13,14},{14,13},{17,18},{18,... | collective-permute-start | bytes 1572872 | tf_op jit(solution)/shard_map/ppermute | solution.py:200
  118.4 29.9 %collective-permute-start.25 = (bf16[512,512]{1,0:T(8,128)(2,1)}, bf16[512,512]{1,0:T(8,128)(2,1)S(1)}, u32[]{:S(2)}, u32[]{:S(2)}) collective-permute-start(bf16[512,512]{1,0:T(8,128)(2,1)} %get-tuple-element.137), channel_id=1, source_target_pairs={{0,1},{1,0},{2,3},{3,2},{4,5},{5,4},{6,7},{7,6},{8,9},{9,8},{10,11... | collective-permute-start | bytes 1572872 | tf_op jit(solution)/shard_map/ppermute | solution.py:200
  124.9 24.4 %collective-permute-start.22 = (bf16[192,2048]{1,0:T(8,128)(2,1)}, bf16[192,2048]{1,0:T(8,128)(2,1)S(1)}, u32[]{:S(2)}, u32[]{:S(2)}) collective-permute-start(bf16[192,2048]{1,0:T(8,128)(2,1)} %get-tuple-element.134), channel_id=1, source_target_pairs={{0,16},{4,20},{8,24},{12,28},{16,0},{20,4},{24,8},{28,12},{1,17},{... | collective-permute-start | bytes 2359304 | tf_op jit(solution)/shard_map/ppermute | solution.py:23
  125.6 23.8 %collective-permute-start.23 = (bf16[192,2048]{1,0:T(8,128)(2,1)}, bf16[192,2048]{1,0:T(8,128)(2,1)S(1)}, u32[]{:S(2)}, u32[]{:S(2)}) collective-permute-start(bf16[192,2048]{1,0:T(8,128)(2,1)} %get-tuple-element.135), channel_id=1, source_target_pairs={{0,8},{4,12},{8,0},{12,4},{16,24},{20,28},{24,16},{28,20},{1,9},{5... | collective-permute-start | bytes 2359304 | tf_op jit(solution)/shard_map/ppermute | solution.py:23
  156.7 22.4 %collective-permute-start.29 = (bf16[512,512]{1,0:T(8,128)(2,1)}, bf16[512,512]{1,0:T(8,128)(2,1)S(1)}, u32[]{:S(2)}, u32[]{:S(2)}) collective-permute-start(bf16[512,512]{1,0:T(8,128)(2,1)} %get-tuple-element.147), channel_id=1, source_target_pairs={{1,2},{2,1},{5,6},{6,5},{9,10},{10,9},{13,14},{14,13},{17,18},{18,... | collective-permute-start | bytes 1572872 | tf_op jit(solution)/shard_map/ppermute | solution.py:200
  157.4 23.2 %collective-permute-start.30 = (bf16[512,512]{1,0:T(8,128)(2,1)S(1)}, bf16[512,512]{1,0:T(8,128)(2,1)S(1)}, u32[]{:S(2)}, u32[]{:S(2)}) collective-permute-start(bf16[512,512]{1,0:T(8,128)(2,1)S(1)} %get-tuple-element.148), channel_id=1, source_target_pairs={{0,1},{1,0},{2,3},{3,2},{4,5},{5,4},{6,7},{7,6},{8,9},{9,8},{10,11... | collective-permute-start | bytes 1572872 | tf_op jit(solution)/shard_map/ppermute | solution.py:200
  169.8 22.0 %collective-permute-start.27 = (bf16[512,512]{1,0:T(8,128)(2,1)S(1)}, bf16[512,512]{1,0:T(8,128)(2,1)S(1)}, u32[]{:S(2)}, u32[]{:S(2)}) collective-permute-start(bf16[512,512]{1,0:T(8,128)(2,1)S(1)} %get-tuple-element.142), channel_id=1, source_target_pairs={{0,1},{1,0},{2,3},{3,2},{4,5},{5,4},{6,7},{7,6},{8,9},{9,8},{10,11... | collective-permute-start | bytes 1572872 | tf_op jit(solution)/shard_map/ppermute | solution.py:200
  172.0 28.0 %collective-permute-start.26 = (bf16[512,512]{1,0:T(8,128)(2,1)S(1)}, bf16[512,512]{1,0:T(8,128)(2,1)S(1)}, u32[]{:S(2)}, u32[]{:S(2)}) collective-permute-start(bf16[512,512]{1,0:T(8,128)(2,1)S(1)} %get-tuple-element.141), channel_id=1, source_target_pairs={{1,2},{2,1},{5,6},{6,5},{9,10},{10,9},{13,14},{14,13},{17,18},{18,... | collective-permute-start | bytes 1572872 | tf_op jit(solution)/shard_map/ppermute | solution.py:200
  181.1 22.1 %collective-permute-start.33 = (bf16[512,512]{1,0:T(8,128)(2,1)S(1)}, bf16[512,512]{1,0:T(8,128)(2,1)S(1)}, u32[]{:S(2)}, u32[]{:S(2)}) collective-permute-start(bf16[512,512]{1,0:T(8,128)(2,1)S(1)} %get-tuple-element.154), channel_id=1, source_target_pairs={{0,1},{1,0},{2,3},{3,2},{4,5},{5,4},{6,7},{7,6},{8,9},{9,8},{10,11... | collective-permute-start | bytes 1572872 | tf_op jit(solution)/shard_map/ppermute | solution.py:200
  183.2 28.1 %collective-permute-start.34 = (bf16[512,512]{1,0:T(8,128)(2,1)S(1)}, bf16[512,512]{1,0:T(8,128)(2,1)S(1)}, u32[]{:S(2)}, u32[]{:S(2)}) collective-permute-start(bf16[512,512]{1,0:T(8,128)(2,1)S(1)} %get-tuple-element.158), channel_id=1, source_target_pairs={{1,2},{2,1},{5,6},{6,5},{9,10},{10,9},{13,14},{14,13},{17,18},{18,... | collective-permute-start | bytes 1572872 | tf_op jit(solution)/shard_map/ppermute | solution.py:200
  213.7 21.0 %collective-permute-start.38 = (bf16[512,512]{1,0:T(8,128)(2,1)S(1)}, bf16[512,512]{1,0:T(8,128)(2,1)S(1)}, u32[]{:S(2)}, u32[]{:S(2)}) collective-permute-start(bf16[512,512]{1,0:T(8,128)(2,1)S(1)} %get-tuple-element.168), channel_id=1, source_target_pairs={{1,2},{2,1},{5,6},{6,5},{9,10},{10,9},{13,14},{14,13},{17,18},{18,... | collective-permute-start | bytes 1572872 | tf_op jit(solution)/shard_map/ppermute | solution.py:200
  (66 other events, 648.8 us)
Sparse Core Ops, SparseCore 0:
  12.0 36.9 all-gather.1

commit v2 on v1

--- a/solution.py
+++ b/solution.py
@@ -555,7 +555,7 @@
     last = ahead + spans - 1 + late
     gathered = rot_act = qin_turned = None
     total = SumOut(outs, core)
-    plan = {2: 2, 4: 2, 6: spans}
+    plan = {2: 2, 4: 2, 5: spans}
     made = 0
     for s in range(last + 1):
         if s == 0:

time: 293 us -> 288 us (0.983)
  local copies, waits for them, and re-layouts: 20.6 us -> 14.8 us
    unnamed x86 -> x76, local copies, waits for them, and re-layouts: 20.4 us -> 14.6 us
    ppermute x26, starting transfers between devices: 41 us -> 37.6 us  [step(): self.got[parity][s] = lax.ppermute(load, self.axis, pairs)]
  transfers between devices with their start and end apart: 47 -> 47, of which waited for: 11 -> 12; matrix products, arithmetic and copies ran while one was open for 0% -> 0% of each run, Pallas kernels for 49% -> 51%
where the time goes in v2:
time: 288 us; the launch traced here: 287 us
  Pallas kernels  156 us (54%)
  starting transfers between devices  55.1 us (19%)
  waiting for transfers between devices  44.6 us (15%)
  local copies, waits for them, and re-layouts  14.8 us (5%)
  between operations  14.7 us (5%)
    pallas_call x33, Pallas kernels, call(): pl.pallas_call(wrapped, in_specs=specs + [ANY] * extra, out_specs=list(ou...  156 us
    ppermute x26, starting transfers between devices, step(): self.got[parity][s] = lax.ppermute(load, self.axis, pairs)  37.6 us
    ppermute x26, waiting for transfers between devices, step(): self.got[parity][s] = lax.ppermute(load, self.axis, pairs)  31.7 us
    ppermute x20, starting transfers between devices, swap(): return lax.ppermute(x, axis, [(i, i ^ bit) for i in range(size)])  17.4 us
    unnamed x76, local copies, waits for them, and re-layouts  14.6 us
    ppermute x20, waiting for transfers between devices, swap(): return lax.ppermute(x, axis, [(i, i ^ bit) for i in range(size)])  12.2 us
  transfers between devices with their start and end apart: 47, of which 12 were waited for; matrix products, arithmetic and copies ran while one was open for 0% of the time, Pallas kernels for 51%

profile of v2, /device:TPU:0, one launch (start us, length us, event | category | flops | bytes accessed | tf_op | source)
XLA Modules:
  0.0 286.6 jit_solution(14882738180618644215)
XLA Ops:
  14.5 7.6 %shard_map.104 = (bf16[512,512]{1,0:T(8,128)(2,1)S(1)}, f32[8,128]{1,0:T(8,128)S(1)}) custom-call(bf16[256,7168]{1,0:T(8,128)(2,1)S(1)} %copy-done.4, bf16[7168,3584]{1,0:T(8,128)(2,1)} %refs_11_.12), custom_call_target="tpu_custom_call" | custom-call | flops 3758096384 | bytes 14680064 | tf_op jit(solution)/shard_map/pallas_call | solution.py:50
  24.6 15.7 %shard_map.106 = (bf16[1536,512]{1,0:T(8,128)(2,1)S(1)}, f32[8,128]{1,0:T(8,128)S(1)}) custom-call(bf16[256,7168]{1,0:T(8,128)(2,1)S(1)} %copy-done.5, bf16[7168,3584]{1,0:T(8,128)(2,1)} %refs_11_.12, f32[8,128]{1,0:T(8,128)S(1)} %get-tuple-element.96.refs_2_), custom_call_target="tpu_custom_call" | custom-call | flops 11274289152 | bytes 44040192 | tf_op jit(solution)/shard_map/pallas_call | solution.py:50
  42.3 8.4 %collective-permute-done.9.refs_3_.refs_7_ = bf16[512,512]{1,0:T(8,128)(2,1)} collective-permute-done((bf16[512,512]{1,0:T(8,128)(2,1)}, bf16[512,512]{1,0:T(8,128)(2,1)}, u32[]{:S(2)}, u32[]{:S(2)}) %collective-permute-start.9) | collective-permute-done | bytes 524320 | tf_op jit(solution)/shard_map/ppermute | solution.py:200
  55.8 6.5 %shard_map.110 = (f32[384,2048]{1,0:T(8,128)}, bf16[384,2048]{1,0:T(8,128)(2,1)}, f32[8,128]{1,0:T(8,128)S(1)}) custom-call(s32[1]{0:T(128)} %bitcast.11.refs_0_, bf16[512,1024]{1,0:T(8,128)(2,1)S(1)} %copy-done.31, bf16[256,1024]{1,0:T(8,128)(2,1)S(1)} %copy-done.32, bf16[1024,2048]{1,0:T(8,128)(2,1)} %refs_3_.1, f32[8,128]{1,0:T(8,128)S(1)} %get-tuple-element.104.refs_4_), custom_call_target="tpu_custom_call" | custom-call | flops 3221225472 | bytes 4194304 | tf_op jit(solution)/shard_map/pallas_call | solution.py:50
  70.2 14.0 %shard_map.111 = (bf16[512,1024]{1,0:T(8,128)(2,1)}, f32[8,128]{1,0:T(8,128)S(1)}) custom-call(s32[10]{0:T(128)S(1)} %stack.43.refs_0_, bf16[64,7168]{1,0:T(8,128)(2,1)S(1)} %copy-done.9, bf16[64,7168]{1,0:T(8,128)(2,1)} %collective-permute-done.refs_2_, bf16[64,7168]{1,0:T(8,128)(2,1)S(1)} %collective-permute-done.1.refs_0_.refs_3_, ...), custom_call_target="tpu_custom_call" | custom-call | flops 7516192768 | bytes 14680064 | tf_op jit(solution)/shard_map/pallas_call | solution.py:50
  85.0 3.3 %shard_map.113 = (bf16[192,2048]{1,0:T(8,128)(2,1)}, bf16[192,2048]{1,0:T(8,128)(2,1)S(1)}, f32[192,2048]{1,0:T(8,128)S(1)}, f32[192,2048]{1,0:T(8,128)S(1)}, f32[8,128]{1,0:T(8,128)S(1)}) custom-call(f32[384,2048]{1,0:T(8,128)} %get-tuple-element.105.refs_0_.refs_1_, f32[384,2048]{1,0:T(8,128)} %get-tuple-element.105.refs_0_.refs_1_, ...), custom_call_target="tpu_custom_call" | custom-call | flops 786432 | bytes 4718592 | tf_op jit(solution)/shard_map/pallas_call | solution.py:50
  94.3 2.7 collective-permute-start.15
  98.8 14.1 %shard_map.115 = (bf16[512,1024]{1,0:T(8,128)(2,1)}, f32[8,128]{1,0:T(8,128)S(1)}) custom-call(s32[10]{0:T(128)S(1)} %stack.43.refs_0_, bf16[64,7168]{1,0:T(8,128)(2,1)S(1)} %copy-done.10, bf16[64,7168]{1,0:T(8,128)(2,1)} %collective-permute-done.refs_2_, bf16[64,7168]{1,0:T(8,128)(2,1)S(1)} %collective-permute-done.1.refs_0_.refs_3_, ...), custom_call_target="tpu_custom_call" | custom-call | flops 7516192768 | bytes 14680064 | tf_op jit(solution)/shard_map/pallas_call | solution.py:50
  116.9 2.7 collective-permute-start.25
  119.7 3.0 %shard_map.117 = (bf16[192,2048]{1,0:T(8,128)(2,1)}, bf16[192,2048]{1,0:T(8,128)(2,1)S(1)}, f32[192,2048]{1,0:T(8,128)S(1)}, f32[192,2048]{1,0:T(8,128)}, f32[8,128]{1,0:T(8,128)S(1)}) custom-call(f32[192,2048]{1,0:T(8,128)} %copy-done.25, f32[192,2048]{1,0:T(8,128)} %copy-done.26, bf16[192,2048]{1,0:T(8,128)(2,1)S(1)} %collective-permute-done.12.refs_2_, ...), custom_call_target="tpu_custom_call" | custom-call | flops 786432 | bytes 4718592 | tf_op jit(solution)/shard_map/pallas_call | solution.py:50
  125.0 18.3 %shard_map.118 = (bf16[512,1536]{1,0:T(8,128)(2,1)}, f32[8,128]{1,0:T(8,128)S(1)}) custom-call(s32[10]{0:T(128)S(1)} %stack.43.refs_0_, bf16[64,7168]{1,0:T(8,128)(2,1)S(1)} %copy-done.10, bf16[64,7168]{1,0:T(8,128)(2,1)} %collective-permute-done.refs_2_, bf16[64,7168]{1,0:T(8,128)(2,1)S(1)} %collective-permute-done.1.refs_0_.refs_3_, ...), custom_call_target="tpu_custom_call" | custom-call | flops 11274289152 | bytes 22020096 | tf_op jit(solution)/shard_map/pallas_call | solution.py:50
  145.7 2.7 shard_map.121
  151.7 2.6 collective-permute-start.30
  154.3 9.4 %collective-permute-done.21.refs_5_.refs_3_.refs_6_ = bf16[512,512]{1,0:T(8,128)(2,1)S(1)} collective-permute-done((bf16[512,512]{1,0:T(8,128)(2,1)S(1)}, bf16[512,512]{1,0:T(8,128)(2,1)S(1)}, u32[]{:S(2)}, u32[]{:S(2)}) %collective-permute-start.21) | collective-permute-done | bytes 524320 | tf_op jit(solution)/shard_map/ppermute | solution.py:200
  169.5 3.9 %shard_map.123 = (bf16[512,2048]{1,0:T(8,128)(2,1)}, bf16[2048,256]{1,0:T(8,128)(2,1)S(1)}, f32[8,128]{1,0:T(8,128)S(1)}) custom-call(s32[1]{0:T(128)} %bitcast.11.refs_0_, bf16[384,2048]{1,0:T(8,128)(2,1)} %bitcast.12.refs_1_, bf16[384,2048]{1,0:T(8,128)(2,1)S(1)} %copy-done.30, f32[8,128]{1,0:T(8,128)S(1)} %get-tuple-element.144.refs_3_), custom_call_target="tpu_custom_call" | custom-call | flops 1572864 | bytes 6291456 | tf_op jit(solution)/shard_map/pallas_call | solution.py:50
  178.2 8.1 %collective-permute-done.27.refs_2_.refs_5_.refs_3_ = bf16[512,512]{1,0:T(8,128)(2,1)S(1)} collective-permute-done((bf16[512,512]{1,0:T(8,128)(2,1)S(1)}, bf16[512,512]{1,0:T(8,128)(2,1)S(1)}, u32[]{:S(2)}, u32[]{:S(2)}) %collective-permute-start.27) | collective-permute-done | bytes 524320 | tf_op jit(solution)/shard_map/ppermute | solution.py:200
  186.3 8.1 %shard_map.125 = (bf16[3584,2048]{1,0:T(8,128)(2,1)}, f32[4,256]{1,0:T(4,128)S(1)}, f32[8,128]{1,0:T(8,128)S(1)}) custom-call(s32[1]{0:T(128)} %bitcast.refs_0_, bf16[512,1024]{1,0:T(8,128)(2,1)S(1)} %copy-done.3, bf16[512,512]{1,0:T(8,128)(2,1)S(1)} %collective-permute-done.27.refs_2_.refs_5_.refs_3_, ...), custom_call_target="tpu_custom_call" | custom-call | flops 4294967296 | bytes 4194304 | tf_op jit(solution)/shard_map/pallas_call | solution.py:50
  198.2 8.2 %shard_map.127 = (bf16[3584,2048]{1,0:T(8,128)(2,1)}, f32[4,256]{1,0:T(4,128)S(1)}, f32[8,128]{1,0:T(8,128)S(1)}) custom-call(s32[1]{0:T(128)} %bitcast.refs_0_, bf16[512,1024]{1,0:T(8,128)(2,1)S(1)} %copy-done.3, bf16[512,512]{1,0:T(8,128)(2,1)S(1)} %collective-permute-done.33.refs_2_.refs_4_.refs_3_, ...), custom_call_target="tpu_custom_call", output_to_operand_aliasing={{0}: (12, {})} | custom-call | flops 4294967296 | bytes 4194304 | tf_op jit(solution)/shard_map/pallas_call | solution.py:50
  210.1 8.1 %shard_map.129 = (bf16[3584,2048]{1,0:T(8,128)(2,1)}, f32[4,256]{1,0:T(4,128)S(1)}, f32[8,128]{1,0:T(8,128)S(1)}) custom-call(s32[1]{0:T(128)} %bitcast.refs_0_, bf16[512,1024]{1,0:T(8,128)(2,1)S(1)} %copy-done.2, bf16[512,512]{1,0:T(8,128)(2,1)S(1)} %collective-permute-done.32.refs_2_.refs_4_.refs_3_, ...), custom_call_target="tpu_custom_call", output_to_operand_aliasing={{0}: (12, {})} | custom-call | flops 4294967296 | bytes 4194304 | tf_op jit(solution)/shard_map/pallas_call | solution.py:50
  221.7 8.2 %shard_map.131 = (bf16[3584,2048]{1,0:T(8,128)(2,1)}, f32[4,256]{1,0:T(4,128)S(1)}, f32[8,128]{1,0:T(8,128)S(1)}) custom-call(s32[1]{0:T(128)} %bitcast.refs_0_, bf16[512,1024]{1,0:T(8,128)(2,1)S(1)} %copy-done.2, bf16[512,512]{1,0:T(8,128)(2,1)S(1)} %collective-permute-done.37.refs_2_, ...), custom_call_target="tpu_custom_call", output_to_operand_aliasing={{0}: (12, {})} | custom-call | flops 4294967296 | bytes 4194304 | tf_op jit(solution)/shard_map/pallas_call | solution.py:50
  232.6 8.1 %shard_map.133 = (bf16[3584,2048]{1,0:T(8,128)(2,1)}, f32[4,256]{1,0:T(4,128)S(1)}, f32[8,128]{1,0:T(8,128)S(1)}) custom-call(s32[1]{0:T(128)} %bitcast.refs_0_, bf16[512,1536]{1,0:T(8,128)(2,1)S(1)} %copy-done.1, bf16[512,512]{1,0:T(8,128)(2,1)S(1)} %collective-permute-done.36.refs_2_, ...), custom_call_target="tpu_custom_call", output_to_operand_aliasing={{0}: (12, {})} | custom-call | flops 4294967296 | bytes 4194304 | tf_op jit(solution)/shard_map/pallas_call | solution.py:50
  241.6 3.3 %collective-permute-done.40.refs_2_ = bf16[512,512]{1,0:T(8,128)(2,1)S(1)} collective-permute-done((bf16[512,512]{1,0:T(8,128)(2,1)S(1)}, bf16[512,512]{1,0:T(8,128)(2,1)S(1)}, u32[]{:S(2)}, u32[]{:S(2)}) %collective-permute-start.40) | collective-permute-done | bytes 524320 | tf_op jit(solution)/shard_map/ppermute | solution.py:200
  244.8 8.3 %shard_map.135 = (bf16[3584,2048]{1,0:T(8,128)(2,1)}, f32[4,256]{1,0:T(4,128)S(1)}, f32[8,128]{1,0:T(8,128)S(1)}) custom-call(s32[1]{0:T(128)} %bitcast.refs_0_, bf16[512,1536]{1,0:T(8,128)(2,1)S(1)} %copy-done.1, bf16[512,512]{1,0:T(8,128)(2,1)S(1)} %collective-permute-done.40.refs_2_, ...), custom_call_target="tpu_custom_call", output_to_operand_aliasing={{0}: (12, {})} | custom-call | flops 4294967296 | bytes 4194304 | tf_op jit(solution)/shard_map/pallas_call | solution.py:50
  254.1 8.1 %shard_map.136 = (bf16[3584,2048]{1,0:T(8,128)(2,1)}, f32[4,256]{1,0:T(4,128)S(1)}, f32[8,128]{1,0:T(8,128)}) custom-call(s32[1]{0:T(128)} %bitcast.refs_0_, bf16[512,1536]{1,0:T(8,128)(2,1)S(1)} %copy-done.1, bf16[512,512]{1,0:T(8,128)(2,1)S(1)} %collective-permute-done.39.refs_2_, ...), custom_call_target="tpu_custom_call", output_to_operand_aliasing={{0}: (12, {})} | custom-call | flops 4294967296 | bytes 4194304 | tf_op jit(solution)/shard_map/pallas_call | solution.py:50
  (195 shorter events, 88.5 us)
Async XLA Ops:
  7.2 46.4 %all-gather.2.cloned.1.call-start = ((), (), s32[]{:S(2)}) async-start(), calls=%async_computation | async-start | bytes 1310720 | tf_op jit(solution)/shard_map/all_gather | solution.py:514
  7.9 54.4 %collective-permute-start = (bf16[64,7168]{1,0:T(8,128)(2,1)}, bf16[64,7168]{1,0:T(8,128)(2,1)}, u32[]{:S(2)}, u32[]{:S(2)}) collective-permute-start(bf16[64,7168]{1,0:T(8,128)(2,1)} %refs_1_.9), channel_id=1, source_target_pairs={{0,4},{4,0},{8,12},{12,8},{16,20},{20,16},{24,28},{28,24},{1,5},{5... | collective-permute-start | bytes 2752520 | tf_op jit(solution)/shard_map/ppermute | solution.py:23
  8.4 32.0 %collective-permute-start.1 = (bf16[64,7168]{1,0:T(8,128)(2,1)}, bf16[64,7168]{1,0:T(8,128)(2,1)S(1)}, u32[]{:S(2)}, u32[]{:S(2)}) collective-permute-start(bf16[64,7168]{1,0:T(8,128)(2,1)} %refs_1_.9), channel_id=1, source_target_pairs={{0,8},{4,12},{8,0},{12,4},{16,24},{20,28},{24,16},{28,20},{1,9},{5... | collective-permute-start | bytes 2752520 | tf_op jit(solution)/shard_map/ppermute | solution.py:23
  11.0 29.4 %collective-permute-start.2 = (bf16[64,7168]{1,0:T(8,128)(2,1)}, bf16[64,7168]{1,0:T(8,128)(2,1)S(1)}, u32[]{:S(2)}, u32[]{:S(2)}) collective-permute-start(bf16[64,7168]{1,0:T(8,128)(2,1)} %refs_1_.9), channel_id=1, source_target_pairs={{0,16},{4,20},{8,24},{12,28},{16,0},{20,4},{24,8},{28,12},{1,17},{... | collective-permute-start | bytes 2752520 | tf_op jit(solution)/shard_map/ppermute | solution.py:23
  23.0 27.6 %collective-permute-start.9 = (bf16[512,512]{1,0:T(8,128)(2,1)}, bf16[512,512]{1,0:T(8,128)(2,1)}, u32[]{:S(2)}, u32[]{:S(2)}) collective-permute-start(bf16[512,512]{1,0:T(8,128)(2,1)} %get-tuple-element.102), channel_id=1, source_target_pairs={{0,1},{1,0},{2,3},{3,2},{4,5},{5,4},{6,7},{7,6},{8,9},{9,8},{10,11... | collective-permute-start | bytes 1572872 | tf_op jit(solution)/shard_map/ppermute | solution.py:200
  41.4 21.4 %collective-permute-start.3 = (bf16[32,7168]{1,0:T(8,128)(2,1)}, bf16[32,7168]{1,0:T(8,128)(2,1)}, u32[]{:S(2)}, u32[]{:S(2)}) collective-permute-start(bf16[32,7168]{1,0:T(8,128)(2,1)} %get-tuple-element.100), channel_id=1, source_target_pairs={{0,8},{4,12},{8,0},{12,4},{16,24},{20,28},{24,16},{28,20},{1,9},{5... | collective-permute-start | bytes 1376264 | tf_op jit(solution)/shard_map/ppermute | solution.py:23
  42.3 21.1 %collective-permute-start.5 = (bf16[64,7168]{1,0:T(8,128)(2,1)S(1)}, bf16[64,7168]{1,0:T(8,128)(2,1)}, u32[]{:S(2)}, u32[]{:S(2)}) collective-permute-start(bf16[64,7168]{1,0:T(8,128)(2,1)S(1)} %collective-permute-done.1.refs_0_.refs_3_), channel_id=1, source_target_pairs={{0,4},{4,0},{8,12},{12,8},{16,20},{20,16},{24,28},{28,24},{1,5},{5... | collective-permute-start | bytes 2752520 | tf_op jit(solution)/shard_map/ppermute | solution.py:23
  62.3 22.1 %collective-permute-start.10 = (bf16[384,2048]{1,0:T(8,128)(2,1)}, bf16[384,2048]{1,0:T(8,128)(2,1)}, u32[]{:S(2)}, u32[]{:S(2)}) collective-permute-start(bf16[384,2048]{1,0:T(8,128)(2,1)} %get-tuple-element.106), channel_id=1, source_target_pairs={{0,4},{4,0},{8,12},{12,8},{16,20},{20,16},{24,28},{28,24},{1,5},{5... | collective-permute-start | bytes 4718600 | tf_op jit(solution)/shard_map/ppermute | solution.py:23
  63.5 30.8 %collective-permute-start.16 = (bf16[512,512]{1,0:T(8,128)(2,1)}, bf16[512,512]{1,0:T(8,128)(2,1)S(1)}, u32[]{:S(2)}, u32[]{:S(2)}) collective-permute-start(bf16[512,512]{1,0:T(8,128)(2,1)} %copy-done.35), channel_id=1, source_target_pairs={{1,2},{2,1},{5,6},{6,5},{9,10},{10,9},{13,14},{14,13},{17,18},{18,... | collective-permute-start | bytes 1572872 | tf_op jit(solution)/shard_map/ppermute | solution.py:200
  66.9 30.1 %collective-permute-start.17 = (bf16[512,512]{1,0:T(8,128)(2,1)}, bf16[512,512]{1,0:T(8,128)(2,1)S(1)}, u32[]{:S(2)}, u32[]{:S(2)}) collective-permute-start(bf16[512,512]{1,0:T(8,128)(2,1)} %copy-done.33), channel_id=1, source_target_pairs={{0,1},{1,0},{2,3},{3,2},{4,5},{5,4},{6,7},{7,6},{8,9},{9,8},{10,11... | collective-permute-start | bytes 1572872 | tf_op jit(solution)/shard_map/ppermute | solution.py:200
  90.7 26.2 %collective-permute-start.12 = (bf16[192,2048]{1,0:T(8,128)(2,1)}, bf16[192,2048]{1,0:T(8,128)(2,1)S(1)}, u32[]{:S(2)}, u32[]{:S(2)}) collective-permute-start(bf16[192,2048]{1,0:T(8,128)(2,1)} %get-tuple-element.113), channel_id=1, source_target_pairs={{0,8},{4,12},{8,0},{12,4},{16,24},{20,28},{24,16},{28,20},{1,9},{5... | collective-permute-start | bytes 2359304 | tf_op jit(solution)/shard_map/ppermute | solution.py:23
  92.1 27.5 %collective-permute-start.13 = (bf16[192,2048]{1,0:T(8,128)(2,1)S(1)}, bf16[192,2048]{1,0:T(8,128)(2,1)S(1)}, u32[]{:S(2)}, u32[]{:S(2)}) collective-permute-start(bf16[192,2048]{1,0:T(8,128)(2,1)S(1)} %get-tuple-element.114), channel_id=1, source_target_pairs={{0,16},{4,20},{8,24},{12,28},{16,0},{20,4},{24,8},{28,12},{1,17},{... | collective-permute-start | bytes 2359304 | tf_op jit(solution)/shard_map/ppermute | solution.py:23
  98.1 26.3 %collective-permute-start.18 = (bf16[512,512]{1,0:T(8,128)(2,1)}, bf16[512,512]{1,0:T(8,128)(2,1)S(1)}, u32[]{:S(2)}, u32[]{:S(2)}) collective-permute-start(bf16[512,512]{1,0:T(8,128)(2,1)} %get-tuple-element.127), channel_id=1, source_target_pairs={{1,2},{2,1},{5,6},{6,5},{9,10},{10,9},{13,14},{14,13},{17,18},{18,... | collective-permute-start | bytes 1572872 | tf_op jit(solution)/shard_map/ppermute | solution.py:200
  112.9 30.4 %collective-permute-start.19 = (bf16[512,512]{1,0:T(8,128)(2,1)}, bf16[512,512]{1,0:T(8,128)(2,1)S(1)}, u32[]{:S(2)}, u32[]{:S(2)}) collective-permute-start(bf16[512,512]{1,0:T(8,128)(2,1)} %get-tuple-element.128), channel_id=1, source_target_pairs={{0,1},{1,0},{2,3},{3,2},{4,5},{5,4},{6,7},{7,6},{8,9},{9,8},{10,11... | collective-permute-start | bytes 1572872 | tf_op jit(solution)/shard_map/ppermute | solution.py:200
  116.0 27.8 %collective-permute-start.24 = (bf16[512,512]{1,0:T(8,128)(2,1)}, bf16[512,512]{1,0:T(8,128)(2,1)S(1)}, u32[]{:S(2)}, u32[]{:S(2)}) collective-permute-start(bf16[512,512]{1,0:T(8,128)(2,1)} %get-tuple-element.136), channel_id=1, source_target_pairs={{1,2},{2,1},{5,6},{6,5},{9,10},{10,9},{13,14},{14,13},{17,18},{18,... | collective-permute-start | bytes 1572872 | tf_op jit(solution)/shard_map/ppermute | solution.py:200
  116.9 26.9 %collective-permute-start.25 = (bf16[512,512]{1,0:T(8,128)(2,1)}, bf16[512,512]{1,0:T(8,128)(2,1)S(1)}, u32[]{:S(2)}, u32[]{:S(2)}) collective-permute-start(bf16[512,512]{1,0:T(8,128)(2,1)} %get-tuple-element.137), channel_id=1, source_target_pairs={{0,1},{1,0},{2,3},{3,2},{4,5},{5,4},{6,7},{7,6},{8,9},{9,8},{10,11... | collective-permute-start | bytes 1572872 | tf_op jit(solution)/shard_map/ppermute | solution.py:200
  123.9 21.8 %collective-permute-start.22 = (bf16[192,2048]{1,0:T(8,128)(2,1)}, bf16[192,2048]{1,0:T(8,128)(2,1)S(1)}, u32[]{:S(2)}, u32[]{:S(2)}) collective-permute-start(bf16[192,2048]{1,0:T(8,128)(2,1)} %get-tuple-element.134), channel_id=1, source_target_pairs={{0,16},{4,20},{8,24},{12,28},{16,0},{20,4},{24,8},{28,12},{1,17},{... | collective-permute-start | bytes 2359304 | tf_op jit(solution)/shard_map/ppermute | solution.py:23
  124.4 21.2 %collective-permute-start.23 = (bf16[192,2048]{1,0:T(8,128)(2,1)S(1)}, bf16[192,2048]{1,0:T(8,128)(2,1)S(1)}, u32[]{:S(2)}, u32[]{:S(2)}) collective-permute-start(bf16[192,2048]{1,0:T(8,128)(2,1)S(1)} %get-tuple-element.135), channel_id=1, source_target_pairs={{0,8},{4,12},{8,0},{12,4},{16,24},{20,28},{24,16},{28,20},{1,9},{5... | collective-permute-start | bytes 2359304 | tf_op jit(solution)/shard_map/ppermute | solution.py:23
  151.0 22.4 %collective-permute-start.29 = (bf16[512,512]{1,0:T(8,128)(2,1)}, bf16[512,512]{1,0:T(8,128)(2,1)S(1)}, u32[]{:S(2)}, u32[]{:S(2)}) collective-permute-start(bf16[512,512]{1,0:T(8,128)(2,1)} %get-tuple-element.147), channel_id=1, source_target_pairs={{1,2},{2,1},{5,6},{6,5},{9,10},{10,9},{13,14},{14,13},{17,18},{18,... | collective-permute-start | bytes 1572872 | tf_op jit(solution)/shard_map/ppermute | solution.py:200
  151.7 23.3 %collective-permute-start.30 = (bf16[512,512]{1,0:T(8,128)(2,1)S(1)}, bf16[512,512]{1,0:T(8,128)(2,1)S(1)}, u32[]{:S(2)}, u32[]{:S(2)}) collective-permute-start(bf16[512,512]{1,0:T(8,128)(2,1)S(1)} %get-tuple-element.148), channel_id=1, source_target_pairs={{0,1},{1,0},{2,3},{3,2},{4,5},{5,4},{6,7},{7,6},{8,9},{9,8},{10,11... | collective-permute-start | bytes 1572872 | tf_op jit(solution)/shard_map/ppermute | solution.py:200
  164.2 22.0 %collective-permute-start.27 = (bf16[512,512]{1,0:T(8,128)(2,1)S(1)}, bf16[512,512]{1,0:T(8,128)(2,1)S(1)}, u32[]{:S(2)}, u32[]{:S(2)}) collective-permute-start(bf16[512,512]{1,0:T(8,128)(2,1)S(1)} %get-tuple-element.142), channel_id=1, source_target_pairs={{0,1},{1,0},{2,3},{3,2},{4,5},{5,4},{6,7},{7,6},{8,9},{9,8},{10,11... | collective-permute-start | bytes 1572872 | tf_op jit(solution)/shard_map/ppermute | solution.py:200
  166.3 28.1 %collective-permute-start.26 = (bf16[512,512]{1,0:T(8,128)(2,1)S(1)}, bf16[512,512]{1,0:T(8,128)(2,1)S(1)}, u32[]{:S(2)}, u32[]{:S(2)}) collective-permute-start(bf16[512,512]{1,0:T(8,128)(2,1)S(1)} %get-tuple-element.141), channel_id=1, source_target_pairs={{1,2},{2,1},{5,6},{6,5},{9,10},{10,9},{13,14},{14,13},{17,18},{18,... | collective-permute-start | bytes 1572872 | tf_op jit(solution)/shard_map/ppermute | solution.py:200
  175.5 22.7 %collective-permute-start.33 = (bf16[512,512]{1,0:T(8,128)(2,1)S(1)}, bf16[512,512]{1,0:T(8,128)(2,1)S(1)}, u32[]{:S(2)}, u32[]{:S(2)}) collective-permute-start(bf16[512,512]{1,0:T(8,128)(2,1)S(1)} %get-tuple-element.154), channel_id=1, source_target_pairs={{0,1},{1,0},{2,3},{3,2},{4,5},{5,4},{6,7},{7,6},{8,9},{9,8},{10,11... | collective-permute-start | bytes 1572872 | tf_op jit(solution)/shard_map/ppermute | solution.py:200
  177.5 28.8 %collective-permute-start.34 = (bf16[512,512]{1,0:T(8,128)(2,1)S(1)}, bf16[512,512]{1,0:T(8,128)(2,1)S(1)}, u32[]{:S(2)}, u32[]{:S(2)}) collective-permute-start(bf16[512,512]{1,0:T(8,128)(2,1)S(1)} %get-tuple-element.158), channel_id=1, source_target_pairs={{1,2},{2,1},{5,6},{6,5},{9,10},{10,9},{13,14},{14,13},{17,18},{18,... | collective-permute-start | bytes 1572872 | tf_op jit(solution)/shard_map/ppermute | solution.py:200
  (61 other events, 625.1 us)
Sparse Core Ops, SparseCore 0:
  9.6 38.9 all-gather.1
